TPU v7x, 32 devices: a whole 2x2x4 slice. The times are simulated.
32 devices in a mesh: ctx: 16 (over z, x, core), tp: 2 (over y).
Axes of the slice: x: 2, y: 2, z: 4, core: 2. Of those that a mesh axis runs over, the one named last changes fastest.
Arguments:
- tokens: bfloat16 [2048, 2048], P('ctx'), may hold values from -6 to 6
- block_ids: int32 [32], replicated, may hold values from 0 to 31, as said below
- gain_attn: bfloat16 [2048], P('ctx'), may hold values from 0.099609375 to 1.8984375
- w_query: bfloat16 [2048, 2048], P('ctx', 'tp'), may hold values from -0.25 to 0.25
- key_weight: bfloat16 [2048, 512], P('ctx', 'tp'), may hold values from -0.125 to 0.125
- value_weight: bfloat16 [2048, 512], P('ctx', 'tp'), may hold values from -0.125 to 0.125
- w_out: bfloat16 [2048, 2048], P('ctx', 'tp'), may hold values from -1 to 1
- gain_mlp: bfloat16 [2048], P('ctx'), may hold values from 0.099609375 to 1.8984375
- w_gate: bfloat16 [2048, 8192], P('ctx', 'tp'), may hold values from -0.125 to 0.125
- w_up: bfloat16 [2048, 8192], P('ctx', 'tp'), may hold values from -0.125 to 0.125
- w_down: bfloat16 [2048, 8192], P('ctx', 'tp'), may hold values from -0.0625 to 0.0625
- cotangent: bfloat16 [2048, 2048], P('ctx'), may hold values from -6 to 6
Outputs:
- block_out: bfloat16 [2048, 2048], P('ctx')
- input_gradient: bfloat16 [2048, 2048], P('ctx')
- gain_attn_gradient: float32 [2048], P('ctx')
- query_gradient: float32 [2048, 2048], P('ctx', 'tp')
- key_gradient: float32 [2048, 512], P('ctx', 'tp')
- value_gradient: float32 [2048, 512], P('ctx', 'tp')
- out_gradient: float32 [2048, 2048], P('ctx', 'tp')
- gain_mlp_gradient: float32 [2048], P('ctx')
- gate_gradient: float32 [2048, 8192], P('ctx', 'tp')
- up_gradient: float32 [2048, 8192], P('ctx', 'tp')
- down_gradient: float32 [2048, 8192], P('ctx', 'tp')
Inputs may be any that keep to these rules, and one draw needn't show every extreme that they name: `block_ids`: each block number 0 to 31 stands once; the two places of one index of ctx hold block numbers that add up to 31.
All inputs are finite; a program needn't handle non-finite values.
Results may differ from a plain program's by a relative error of at most 0.019.
The roundings to bfloat16 on the way count: a program that leaves them out, or rounds other values in their place, can miss the bound.
Values may be sent and summed in bfloat16 or wider, within the bound.
A program may use at most 576 MiB of HBM per device.

v0:
```python
import math

import jax
import jax.numpy as jnp
from jax import lax
from jax.sharding import PartitionSpec as P

HEAD_DIM = 64
BLOCK = 64


EPS = 1e-05
THETA = 500000.0
NEG = -1e30


def turned(tensor):
    half_width = tensor.shape[-1] // 2
    return jnp.concatenate([-tensor[..., half_width:], tensor[..., :half_width]], axis=-1)


def rotary_embed(tensor, cosine_table, sine_table):
    return tensor * cosine_table[:, None, :] + turned(tensor) * sine_table[:, None, :]


def rope_tables(token_positions, head_width):
    half_width = head_width // 2
    frequencies = THETA ** (-(jnp.arange(half_width, dtype=jnp.float32) * 2.0 / head_width))
    angles = token_positions.astype(jnp.float32)[:, None] * frequencies[None, :]
    angles = jnp.concatenate([angles, angles], axis=1)
    return (jnp.cos(angles), jnp.sin(angles))


def norm_back(grad_norm, scaled, factor, gain_vec):
    weighted = grad_norm * gain_vec[None, :]
    return factor * (weighted - scaled * jnp.mean(weighted * scaled, axis=1, keepdims=True))


def local(
    tokens,
    block_ids,
    gain_attn,
    w_query,
    key_weight,
    value_weight,
    w_out,
    gain_mlp,
    w_gate,
    w_up,
    w_down,
    cotangent,
):
    row_count, model_width = tokens.shape
    sequence_length = row_count * lax.axis_size("ctx")
    query_cols = w_query.shape[1]
    kv_cols = key_weight.shape[1]
    hidden_cols = w_gate.shape[1]
    kv_heads = kv_cols // HEAD_DIM
    group_length = query_cols // kv_cols
    key_block = math.gcd(sequence_length, 1024)
    block_count = sequence_length // key_block
    score_scale = HEAD_DIM ** (-0.5)
    attn_width = 2 * query_cols + 2 * kv_cols
    offsets = jnp.arange(BLOCK, dtype=jnp.int32)
    all_positions = (block_ids[:, None] * BLOCK + offsets[None, :]).reshape(sequence_length)
    token_positions = lax.dynamic_slice_in_dim(
        all_positions, lax.axis_index("ctx") * row_count, row_count
    )
    cosine_table, sine_table = rope_tables(token_positions, HEAD_DIM)
    inputs = tokens.astype(jnp.float32)
    factor_attn = lax.rsqrt(jnp.mean(inputs * inputs, axis=1, keepdims=True) + EPS)
    scaled_attn = inputs * factor_attn
    slab_query = lax.all_gather(w_query, "ctx", axis=0, tiled=True)
    slab_key = lax.all_gather(key_weight, "ctx", axis=0, tiled=True)
    slab_value = lax.all_gather(value_weight, "ctx", axis=0, tiled=True)
    slab_out = lax.all_gather(w_out, "ctx", axis=0, tiled=True)
    slab_gain = lax.all_gather(gain_attn, "ctx", axis=0, tiled=True)
    normed = (scaled_attn * slab_gain.astype(jnp.float32)[None, :]).astype(jnp.bfloat16)
    acc_query = jnp.dot(normed, slab_query, preferred_element_type=jnp.float32)
    acc_key = jnp.dot(normed, slab_key, preferred_element_type=jnp.float32)
    acc_value = jnp.dot(normed, slab_value, preferred_element_type=jnp.float32)
    full_query = slab_query
    full_key = slab_key
    full_value = slab_value
    full_out = slab_out
    full_gain = slab_gain
    (
        query_lin,
        key_linear,
        value_linear,
        full_query,
        full_key,
        full_value,
        full_out,
        full_gain_attn,
    ) = (acc_query, acc_key, acc_value, full_query, full_key, full_value, full_out, full_gain)
    query_rotated = rotary_embed(
        query_lin.reshape(row_count, -1, HEAD_DIM), cosine_table, sine_table
    ).astype(jnp.bfloat16)
    key_rotated = (
        rotary_embed(key_linear.reshape(row_count, kv_heads, HEAD_DIM), cosine_table, sine_table)
        .astype(jnp.bfloat16)
        .reshape(row_count, kv_cols)
    )
    value_low = value_linear.astype(jnp.bfloat16)
    keys_all, values_all = (
        lax.all_gather(key_rotated, "ctx", axis=0, tiled=True),
        lax.all_gather(value_low, "ctx", axis=0, tiled=True),
    )
    key_blocks = keys_all.reshape(block_count, key_block, kv_heads, HEAD_DIM)
    value_blocks = values_all.reshape(block_count, key_block, kv_heads, HEAD_DIM)
    pos_blocks = all_positions.reshape(block_count, key_block)
    queries = query_rotated.reshape(row_count, kv_heads, group_length, HEAD_DIM)

    def scores_of(key_part, pos_part):
        raw_scores = (
            jnp.einsum("qkgd,skd->kgqs", queries, key_part, preferred_element_type=jnp.float32)
            * score_scale
        )
        allowed = pos_part[None, :] <= token_positions[:, None]
        return jnp.where(allowed[None, None], raw_scores, NEG)

    def max_step(totals, blocks):
        run_max, run_sum = totals
        key_part, pos_part = blocks
        scores = scores_of(key_part, pos_part)
        new_max = jnp.maximum(run_max, jnp.max(scores, axis=-1, keepdims=True))
        run_sum = run_sum * jnp.exp(run_max - new_max) + jnp.sum(
            jnp.exp(scores - new_max), axis=-1, keepdims=True
        )
        return ((new_max, run_sum), None)

    stat_shape = (kv_heads, group_length, row_count, 1)
    (row_max, row_sum), unused = lax.scan(
        max_step,
        (jnp.full(stat_shape, NEG, jnp.float32), jnp.zeros(stat_shape, jnp.float32)),
        (key_blocks, pos_blocks),
    )

    def softmax_of(scores):
        return jnp.exp(scores - row_max) / row_sum

    def out_step(totals, blocks):
        key_part, value_part, pos_part = blocks
        softmaxed = softmax_of(scores_of(key_part, pos_part)).astype(jnp.bfloat16)
        return (
            totals
            + jnp.einsum(
                "kgqs,skd->qkgd", softmaxed, value_part, preferred_element_type=jnp.float32
            ),
            None,
        )

    mixed_full, unused = lax.scan(
        out_step,
        jnp.zeros((row_count, kv_heads, group_length, HEAD_DIM), jnp.float32),
        (key_blocks, value_blocks, pos_blocks),
    )
    mixed_heads = mixed_full.astype(jnp.bfloat16).reshape(row_count, query_cols)
    attn_part = jnp.einsum("rc,dc->rd", mixed_heads, full_out, preferred_element_type=jnp.float32)
    attn_out = lax.psum(attn_part.astype(jnp.bfloat16), "tp").astype(jnp.float32)
    residual = inputs + attn_out
    factor_mlp = lax.rsqrt(jnp.mean(residual * residual, axis=1, keepdims=True) + EPS)
    scaled_mlp = residual * factor_mlp
    slab_gate = lax.all_gather(w_gate, "ctx", axis=0, tiled=True)
    slab_up = lax.all_gather(w_up, "ctx", axis=0, tiled=True)
    slab_gain = lax.all_gather(gain_mlp, "ctx", axis=0, tiled=True)
    normed = (scaled_mlp * slab_gain.astype(jnp.float32)[None, :]).astype(jnp.bfloat16)
    acc_gate = jnp.dot(normed, slab_gate, preferred_element_type=jnp.float32)
    acc_up = jnp.dot(normed, slab_up, preferred_element_type=jnp.float32)
    full_gain = slab_gain
    sigmoid_gate = jax.nn.sigmoid(acc_gate)
    silu_gate = acc_gate * sigmoid_gate
    hidden = (silu_gate * acc_up).astype(jnp.bfloat16)
    mlp_part = jnp.einsum(
        "rf,df->rd",
        hidden,
        lax.all_gather(w_down, "ctx", axis=0, tiled=True),
        preferred_element_type=jnp.float32,
    )
    mlp_out = lax.psum(mlp_part.astype(jnp.bfloat16), "tp").astype(jnp.float32)
    block_out = (residual + mlp_out).astype(jnp.bfloat16)
    grad_full = cotangent.astype(jnp.float32)
    grad_hidden = jnp.dot(
        cotangent,
        lax.all_gather(w_down, "ctx", axis=0, tiled=True),
        preferred_element_type=jnp.float32,
    )
    grad_gate = (
        grad_hidden * acc_up * sigmoid_gate * (1.0 + acc_gate * (1.0 - sigmoid_gate))
    ).astype(jnp.bfloat16)
    grad_up = (grad_hidden * silu_gate).astype(jnp.bfloat16)
    gain_mlp_full = full_gain.astype(jnp.float32)
    slab_gate, slab_up = lax.all_gather((w_gate, w_up), "ctx", axis=0, tiled=True)
    grad_norm_part = jnp.einsum(
        "rf,df->rd", grad_gate, slab_gate, preferred_element_type=jnp.float32
    ) + jnp.einsum("rf,df->rd", grad_up, slab_up, preferred_element_type=jnp.float32)
    grad_norm_mlp = lax.psum(grad_norm_part.astype(jnp.bfloat16), "tp").astype(jnp.float32)
    grad_residual = grad_full + norm_back(grad_norm_mlp, scaled_mlp, factor_mlp, gain_mlp_full)
    grad_attn = grad_residual.astype(jnp.bfloat16)
    grad_mixed = jnp.dot(grad_attn, full_out, preferred_element_type=jnp.float32).astype(
        jnp.bfloat16
    )
    grad_mixed_heads = grad_mixed.reshape(row_count, kv_heads, group_length, HEAD_DIM)
    row_delta = jnp.sum(grad_mixed_heads.astype(jnp.float32) * mixed_full, axis=-1)
    row_delta = jnp.transpose(row_delta, (1, 2, 0))[..., None]

    def grad_step(totals, blocks):
        key_part, value_part, pos_part = blocks
        softmaxed = softmax_of(scores_of(key_part, pos_part))
        grad_probs = jnp.einsum(
            "qkgd,skd->kgqs", grad_mixed_heads, value_part, preferred_element_type=jnp.float32
        )
        grad_scores = (softmaxed * (grad_probs - row_delta)).astype(jnp.bfloat16)
        totals = (
            totals
            + jnp.einsum(
                "kgqs,skd->qkgd", grad_scores, key_part, preferred_element_type=jnp.float32
            )
            * score_scale
        )
        grad_keys = (
            jnp.einsum("kgqs,qkgd->skd", grad_scores, queries, preferred_element_type=jnp.float32)
            * score_scale
        )
        grad_values = jnp.einsum(
            "kgqs,qkgd->skd",
            softmaxed.astype(jnp.bfloat16),
            grad_mixed_heads,
            preferred_element_type=jnp.float32,
        )
        return (totals, (grad_keys, grad_values))

    grad_query_full, (grad_key_blocks, grad_value_blocks) = lax.scan(
        grad_step,
        jnp.zeros((row_count, kv_heads, group_length, HEAD_DIM), jnp.float32),
        (key_blocks, value_blocks, pos_blocks),
    )
    grad_key_own, grad_value_own = (
        lax.psum_scatter(
            grad_key_blocks.reshape(sequence_length, kv_cols),
            "ctx",
            scatter_dimension=0,
            tiled=True,
        ),
        lax.psum_scatter(
            grad_value_blocks.reshape(sequence_length, kv_cols),
            "ctx",
            scatter_dimension=0,
            tiled=True,
        ),
    )
    grad_query = (
        rotary_embed(grad_query_full.reshape(row_count, -1, HEAD_DIM), cosine_table, -sine_table)
        .astype(jnp.bfloat16)
        .reshape(row_count, query_cols)
    )
    grad_key = (
        rotary_embed(grad_key_own.reshape(row_count, kv_heads, HEAD_DIM), cosine_table, -sine_table)
        .astype(jnp.bfloat16)
        .reshape(row_count, kv_cols)
    )
    grad_value = grad_value_own.astype(jnp.bfloat16)
    grad_norm_local = (
        jnp.einsum("rc,dc->rd", grad_query, full_query, preferred_element_type=jnp.float32)
        + jnp.einsum("rc,dc->rd", grad_key, full_key, preferred_element_type=jnp.float32)
        + jnp.einsum("rc,dc->rd", grad_value, full_value, preferred_element_type=jnp.float32)
    )
    grad_norm_attn = lax.psum(grad_norm_local.astype(jnp.bfloat16), "tp").astype(jnp.float32)
    gain_attn_full = full_gain_attn.astype(jnp.float32)
    input_gradient = (
        grad_residual + norm_back(grad_norm_attn, scaled_attn, factor_attn, gain_attn_full)
    ).astype(jnp.bfloat16)
    gain_attn_gradient, gain_mlp_gradient = (
        lax.psum_scatter(
            jnp.sum(grad_norm_attn * scaled_attn, axis=0), "ctx", scatter_dimension=0, tiled=True
        ),
        lax.psum_scatter(
            jnp.sum(grad_norm_mlp * scaled_mlp, axis=0), "ctx", scatter_dimension=0, tiled=True
        ),
    )
    normed = (scaled_mlp * gain_mlp_full[None, :]).astype(jnp.bfloat16)
    attn_normed = (scaled_attn * gain_attn_full[None, :]).astype(jnp.bfloat16)
    summed_terms = lax.psum_scatter(
        jnp.concatenate(
            [
                jnp.concatenate(
                    [
                        jnp.einsum(
                            "rn,rc->nc", attn_normed, grad_query, preferred_element_type=jnp.float32
                        ),
                        jnp.einsum(
                            "rn,rc->nc", attn_normed, grad_key, preferred_element_type=jnp.float32
                        ),
                        jnp.einsum(
                            "rn,rc->nc", attn_normed, grad_value, preferred_element_type=jnp.float32
                        ),
                        jnp.einsum(
                            "rn,rc->nc", grad_attn, mixed_heads, preferred_element_type=jnp.float32
                        ),
                    ],
                    axis=1,
                ),
                jnp.concatenate(
                    [
                        jnp.einsum(
                            "rn,rf->nf", normed, grad_gate, preferred_element_type=jnp.float32
                        ),
                        jnp.einsum(
                            "rn,rf->nf", normed, grad_up, preferred_element_type=jnp.float32
                        ),
                        jnp.einsum(
                            "rn,rf->nf", cotangent, hidden, preferred_element_type=jnp.float32
                        ),
                    ],
                    axis=1,
                ),
            ],
            axis=1,
        ),
        "ctx",
        scatter_dimension=0,
        tiled=True,
    )
    mlp_summed = summed_terms[:, attn_width:]
    query_gradient = summed_terms[:, :query_cols]
    key_gradient = summed_terms[:, query_cols : query_cols + kv_cols]
    value_gradient = summed_terms[:, query_cols + kv_cols : query_cols + 2 * kv_cols]
    out_gradient = summed_terms[:, query_cols + 2 * kv_cols : attn_width]
    gate_gradient = mlp_summed[:, :hidden_cols]
    up_gradient = mlp_summed[:, hidden_cols : 2 * hidden_cols]
    down_gradient = mlp_summed[:, 2 * hidden_cols : 3 * hidden_cols]
    return (
        block_out,
        input_gradient,
        gain_attn_gradient,
        query_gradient,
        key_gradient,
        value_gradient,
        out_gradient,
        gain_mlp_gradient,
        gate_gradient,
        up_gradient,
        down_gradient,
    )


def solution(mesh):
    placed = (
        P("ctx", None),
        P(),
        P("ctx"),
        P("ctx", "tp"),
        P("ctx", "tp"),
        P("ctx", "tp"),
        P("ctx", "tp"),
        P("ctx"),
        P("ctx", "tp"),
        P("ctx", "tp"),
        P("ctx", "tp"),
        P("ctx", None),
    )
    return jax.shard_map(
        local,
        mesh=mesh,
        in_specs=placed,
        out_specs=(
            P("ctx", None),
            P("ctx", None),
            P("ctx"),
            P("ctx", "tp"),
            P("ctx", "tp"),
            P("ctx", "tp"),
            P("ctx", "tp"),
            P("ctx"),
            P("ctx", "tp"),
            P("ctx", "tp"),
            P("ctx", "tp"),
        ),
        check_vma=False,
    )
```

profile of v0, /device:TPU:1, one launch (start us, length us, event | category | flops | bytes accessed | tf_op | source)
XLA Modules:
  0.0 3108.5 jit_solution(8811685422250163795)
XLA Ops:
  9.4 23.0 all-gather
  34.7 15.9 all-gather.16.cloned.1.call-done
  53.4 36.3 %all-gather.12.cloned.1.call-done = bf16[2048,256]{1,0:T(8,128)(2,1)} async-done(((bf16[128,256]{1,0:T(8,128)(2,1)}), bf16[2048,256]{1,0:T(8,128)(2,1)}) %all-gather.12.cloned.1.call-update) | async-done | bytes 1048592 | tf_op jit(solution)/shard_map/all_gather | solution.py:75
  89.7 2.4 convolution_convert_fusion.3
  93.6 35.7 %all-gather.18.cloned.1.call-done = bf16[2048,256]{1,0:T(8,128)(2,1)} async-done(((bf16[128,256]{1,0:T(8,128)(2,1)}), bf16[2048,256]{1,0:T(8,128)(2,1)}) %all-gather.18.cloned.1.call-update) | async-done | bytes 1048592 | tf_op jit(solution)/shard_map/all_gather | solution.py:107
  129.3 4.4 reshape.290
  133.8 2.9 copy.82
  136.7 32.1 %all-gather.14.cloned.1.call-done = bf16[2048,256]{1,0:T(8,128)(2,1)} async-done(((bf16[128,256]{1,0:T(8,128)(2,1)}), bf16[2048,256]{1,0:T(8,128)(2,1)}) %all-gather.14.cloned.1.call-update) | async-done | bytes 1048592 | tf_op jit(solution)/shard_map/all_gather | solution.py:108
  168.8 4.4 reshape.289
  173.2 4.0 copy.81
  177.3 43.1 %all-gather.20.cloned.1.call-done = bf16[2048,1024]{1,0:T(8,128)(2,1)} async-done(((bf16[128,1024]{1,0:T(8,128)(2,1)}), bf16[2048,1024]{1,0:T(8,128)(2,1)}) %all-gather.20.cloned.1.call-update) | async-done | bytes 4194320 | tf_op jit(solution)/shard_map/all_gather | solution.py:73
  220.3 4.0 fusion.90
  224.5 6.7 while.39
  231.1 8.6 while.40
  231.4 4.0 fusion.173
  235.7 4.0 fusion.173
  239.8 31.7 %all-gather.22.cloned.1.call-done = bf16[2048,1024]{1,0:T(8,128)(2,1)} async-done(((bf16[128,1024]{1,0:T(8,128)(2,1)}), bf16[2048,1024]{1,0:T(8,128)(2,1)}) %all-gather.22.cloned.1.call-update) | async-done | bytes 4194320 | tf_op jit(solution)/shard_map/all_gather | solution.py:76
  271.5 4.5 convolution_convert_fusion.1
  278.1 19.1 all-gather.1
  297.2 5.6 all-reduce.10.cloned.1.call-done
  305.4 127.1 %all-gather.26.cloned.1.call-done = bf16[2048,4096]{1,0:T(8,128)(2,1)} async-done(((bf16[128,4096]{1,0:T(8,128)(2,1)}), bf16[2048,4096]{1,0:T(8,128)(2,1)}) %all-gather.26.cloned.1.call-update) | async-done | bytes 16777232 | tf_op jit(solution)/shard_map/all_gather | solution.py:166
  432.6 9.4 fusion.102
  442.0 118.1 %all-gather.24.cloned.1.call-done = bf16[2048,4096]{1,0:T(8,128)(2,1)} async-done(((bf16[128,4096]{1,0:T(8,128)(2,1)}), bf16[2048,4096]{1,0:T(8,128)(2,1)}) %all-gather.24.cloned.1.call-update) | async-done | bytes 16777232 | tf_op jit(solution)/shard_map/all_gather | solution.py:165
  560.0 9.4 fusion.101
  569.5 117.9 %all-gather.28.cloned.1.call-done = bf16[2048,4096]{1,0:T(8,128)(2,1)} async-done(((bf16[128,4096]{1,0:T(8,128)(2,1)}), bf16[2048,4096]{1,0:T(8,128)(2,1)}) %all-gather.28.cloned.1.call-update) | async-done | bytes 16777232 | tf_op jit(solution)/shard_map/all_gather | solution.py:178
  687.4 12.2 multiply_convert_fusion
  699.6 24.0 fusion.103
  723.6 12.8 fusion.53
  736.5 26.4 all-reduce.12.cloned.1.call-done
  763.0 2.1 fusion.69
  765.1 4.1 convolution_convert_fusion.2
  769.2 1.8 copy.83
  772.0 101.6 %while.41 = (s32[]{:T(128)}, f32[128,4,4,64]{0,3,2,1:T(8,128)}, f32[2,1024,4,64]{1,0,3,2:T(2,128)}, f32[2,1024,4,64]{1,0,3,2:T(2,128)}, bf16[2,1024,4,64]{1,3,2,...) while((s32[]{:T(128)}, f32[128,4,4,64]{0,3,2,1:T(8,128)}, ...), condition=%wide.region_14.15_spmd.clone, body=%wide.region_13.14_spmd.clone.sunk | while | flops 1359740928 | bytes 52204212 | solution.py:234
  772.3 2.5 fusion.184
  774.8 2.3 fusion.188
  777.1 2.5 fusion.185
  784.8 18.8 dynamic_update_slice.11
  803.6 18.8 dynamic_update_slice.12
  822.5 2.5 fusion.184
  825.0 2.3 fusion.188
  827.4 2.4 fusion.185
  830.9 2.7 fusion.186
  836.1 18.8 dynamic_update_slice.11
  854.9 18.8 dynamic_update_slice.12
  873.6 3.9 copy.125
  877.6 3.8 copy.126
  881.7 12.6 convolution_convert_fusion
  897.4 4.7 convolution_dynamic-update-slice_fusion.3
  902.1 35.6 %reduce-scatter.3.cloned.1.call-done = f32[128,256]{0,1:T(8,128)} async-done(((f32[2048,256]{0,1:T(8,128)}), f32[128,256]{0,1:T(8,128)}) %reduce-scatter.3.cloned.1.call-update) | async-done | bytes 131088 | tf_op jit(solution)/shard_map/reduce_scatter | solution.py:240
  939.5 1.9 convolution_dynamic-update-slice_fusion.5
  941.5 61.6 %reduce-scatter.5.cloned.1.call-done = f32[128,256]{0,1:T(8,128)} async-done(((f32[2048,256]{0,1:T(8,128)}), f32[128,256]{0,1:T(8,128)}) %reduce-scatter.5.cloned.1.call-update) | async-done | bytes 131088 | tf_op jit(solution)/shard_map/reduce_scatter | solution.py:246
  1003.1 2.9 convolution_dynamic-update-slice_fusion.4
  1006.1 4.8 convolution_dynamic-update-slice_fusion.2
  1010.9 13.5 convolution_dynamic-update-slice_fusion.1
  1024.4 13.3 convolution_dynamic-update-slice_fusion
  1038.7 2.3 fusion.54
  1041.1 13.7 bitcast_dynamic-update-slice_fusion
  1056.7 25.3 all-reduce.16.cloned.1.call-done
  1083.5 59.7 %all-reduce.3 = (f32[2048]{0:T(1024)S(1)}, f32[2048]{0:T(1024)S(1)}) all-reduce(f32[2048]{0:T(1024)S(1)} %get-tuple-element.356, f32[2048]{0:T(1024)S(1)} %copy-done.27), channel_id=4, replica_groups=mesh['ctx'=16,'tp'=2] {'ctx'}, use_global_device_ids=true, to_apply=%region_20.21.clone | all-reduce | flops 4096 | bytes 32768
  1144.4 3.0 fusion.65
  1147.4 1942.6 %all-reduce.14.cloned.1.call-done = f32[2048,14848]{1,0:T(8,128)} async-done(((f32[2048,14848]{1,0:T(8,128)}), f32[2048,14848]{1,0:T(8,128)}) %all-reduce.14.cloned.1.call-update) | async-done | bytes 121634832
  3090.0 2.4 fusion.99
  3092.4 1.9 fusion.100
  3094.2 7.3 fusion.98
  (183 shorter events, 40.9 us)
Async XLA Ops:
  7.2 43.5 %all-gather.16.cloned.1.call-start = ((), (), s32[]{:S(2)}) async-start(), calls=%async_computation.4 | async-start | bytes 1114112 | tf_op jit(solution)/shard_map/all_gather | solution.py:74
  7.9 81.8 %all-gather.12.cloned.1.call-start = ((), (), s32[]{:S(2)}) async-start(), calls=%async_computation.2 | async-start | bytes 1114112 | tf_op jit(solution)/shard_map/all_gather | solution.py:75
  8.7 120.7 %all-gather.18.cloned.1.call-start = ((), (), s32[]{:S(2)}) async-start(), calls=%async_computation.5 | async-start | bytes 1114112 | tf_op jit(solution)/shard_map/all_gather | solution.py:107
  32.4 187.9 %copy-start.21 = (f32[16,1,128]{2,1,0:T(1,128)}, f32[16,1,128]{2,1,0:T(1,128)S(1)}, u32[]{:S(2)}) copy-start(f32[16,1,128]{2,1,0:T(1,128)S(1)} %convert_element_type.137) | copy-start | bytes 24580
  33.4 191.0 %copy-start.19 = (f32[128,64]{0,1:T(8,128)}, f32[128,64]{0,1:T(8,128)S(1)}, u32[]{:S(2)}) copy-start(f32[128,64]{0,1:T(8,128)S(1)} %get-tuple-element.446) | copy-start | bytes 98308
  34.7 185.6 %copy-start.28 = (f32[128]{0:T(128)}, f32[128]{0:T(128)S(1)}, u32[]{:S(2)}) copy-start(f32[128]{0:T(128)S(1)} %add_rsqrt_fusion.1) | copy-start | bytes 1540
  52.4 167.9 %copy-start = (bf16[128,2048]{1,0:T(8,128)(2,1)S(1)}, bf16[128,2048]{1,0:T(8,128)(2,1)}, u32[]{:S(2)}) copy-start(bf16[128,2048]{1,0:T(8,128)(2,1)} %param.18) | copy-start | bytes 1572868
  53.3 115.5 %all-gather.14.cloned.1.call-start = ((), (), s32[]{:S(2)}) async-start(), calls=%async_computation.3 | async-start | bytes 1114112 | tf_op jit(solution)/shard_map/all_gather | solution.py:108
  92.1 128.2 %all-gather.20.cloned.1.call-start = ((), (), s32[]{:S(2)}) async-start(), calls=%async_computation.6 | async-start | bytes 4456448 | tf_op jit(solution)/shard_map/all_gather | solution.py:73
  92.7 178.8 %all-gather.22.cloned.1.call-start = ((), (), s32[]{:S(2)}) async-start(), calls=%async_computation.7 | async-start | bytes 4456448 | tf_op jit(solution)/shard_map/all_gather | solution.py:76
  93.3 209.5 %all-reduce.10.cloned.1.call-start = ((), (), s32[]{:S(2)}) async-start(), calls=%async_computation.8 | async-start | bytes 1048576 | tf_op jit(solution)/shard_map/psum | solution.py:161
  239.7 38.4 %copy-start.34 = (bf16[128]{0:T(256)(128)(2,1)S(1)}, bf16[128]{0:T(256)(128)(2,1)}, u32[]{:S(2)}) copy-start(bf16[128]{0:T(256)(128)(2,1)} %param.25) | copy-start | bytes 772
  239.8 64.3 %copy-start.13 = (bf16[128,4,4,64]{0,3,2,1:T(8,128)(2,1)}, bf16[128,4,4,64]{0,3,2,1:T(8,128)(2,1)S(1)}, u32[]{:S(2)}) copy-start(bf16[128,4,4,64]{0,3,2,1:T(8,128)(2,1)S(1)} %convert_element_type.114) | copy-start | bytes 786436
  276.0 156.6 %all-gather.26.cloned.1.call-start = ((), (), s32[]{:S(2)}) async-start(), calls=%async_computation.10 | async-start | bytes 17825792 | tf_op jit(solution)/shard_map/all_gather | solution.py:166
  276.7 283.3 %all-gather.24.cloned.1.call-start = ((), (), s32[]{:S(2)}) async-start(), calls=%async_computation.9 | async-start | bytes 17825792 | tf_op jit(solution)/shard_map/all_gather | solution.py:165
  277.5 409.9 %all-gather.28.cloned.1.call-start = ((), (), s32[]{:S(2)}) async-start(), calls=%async_computation.11 | async-start | bytes 17825792 | tf_op jit(solution)/shard_map/all_gather | solution.py:178
  278.1 484.9 %all-reduce.12.cloned.1.call-start = ((), (), s32[]{:S(2)}) async-start(), calls=%async_computation.12 | async-start | bytes 1048576 | tf_op jit(solution)/shard_map/psum | solution.py:198
  297.2 467.9 %copy-start.24 = (f32[16,1,128]{2,1,0:T(1,128)}, f32[16,1,128]{2,1,0:T(1,128)S(1)}, u32[]{:S(2)}) copy-start(f32[16,1,128]{2,1,0:T(1,128)S(1)} %convert_element_type.138) | copy-start | bytes 24580
  304.1 461.0 %copy-start.30 = (f32[128]{0:T(128)}, f32[128]{0:T(128)S(1)}, u32[]{:S(2)}) copy-start(f32[128]{0:T(128)S(1)} %add_rsqrt_fusion) | copy-start | bytes 1540
  305.4 254.6 %copy-start.2 = (bf16[128,2048]{1,0:T(8,128)(2,1)}, bf16[128,2048]{1,0:T(8,128)(2,1)S(1)}, u32[]{:S(2)}) copy-start(bf16[128,2048]{1,0:T(8,128)(2,1)S(1)} %multiply_convert_fusion.3) | copy-start | bytes 1572868
  442.0 245.4 %copy-start.7 = (bf16[128,2048]{1,0:T(8,128)(2,1)S(1)}, bf16[128,2048]{1,0:T(8,128)(2,1)}, u32[]{:S(2)}) copy-start(bf16[128,2048]{1,0:T(8,128)(2,1)} %param.29) | copy-start | bytes 1572868
  723.6 39.4 %copy-start.5 = (bf16[128,2048]{1,0:T(8,128)(2,1)S(1)}, bf16[128,2048]{1,0:T(8,128)(2,1)}, u32[]{:S(2)}) copy-start(bf16[128,2048]{1,0:T(8,128)(2,1)} %all-reduce.10.cloned.1.call-done) | copy-start | bytes 1572868
  736.5 201.2 %reduce-scatter.3.cloned.1.call-start = ((), (), s32[]{:S(2)}) async-start(), calls=%async_computation.13 | async-start | bytes 2228224 | tf_op jit(solution)/shard_map/reduce_scatter | solution.py:240
  765.1 6.9 copy-start.32
  873.6 8.0 copy-start.10
  877.5 125.6 %reduce-scatter.5.cloned.1.call-start = ((), (), s32[]{:S(2)}) async-start(), calls=%async_computation.14 | async-start | bytes 2228224 | tf_op jit(solution)/shard_map/reduce_scatter | solution.py:246
  881.4 200.6 %all-reduce.16.cloned.1.call-start = ((), (), s32[]{:S(2)}) async-start(), calls=%async_computation.16 | async-start | bytes 2097152 | tf_op jit(solution)/shard_map/psum | solution.py:181
  881.7 13.8 copy-start.26
  881.7 13.8 copy-start.20
  881.7 15.7 copy-start.1
  881.7 15.7 copy-start.22
  881.7 15.7 copy-start.29
  896.6 0.7 copy-start.15
  897.4 108.7 %copy-start.6 = (bf16[128,2048]{1,0:T(8,128)(2,1)S(1)}, bf16[128,2048]{1,0:T(8,128)(2,1)}, u32[]{:S(2)}) copy-start(bf16[128,2048]{1,0:T(8,128)(2,1)} %all-reduce.10.cloned.1.call-done) | copy-start | bytes 1572868
  897.4 108.7 %copy-start.8 = (bf16[128,2048]{1,0:T(8,128)(2,1)S(1)}, bf16[128,2048]{1,0:T(8,128)(2,1)}, u32[]{:S(2)}) copy-start(bf16[128,2048]{1,0:T(8,128)(2,1)} %param.29) | copy-start | bytes 1572868
  897.4 108.6 %copy-start.9 = (bf16[128,2048]{1,0:T(8,128)(2,1)S(1)}, bf16[128,2048]{1,0:T(8,128)(2,1)}, u32[]{:S(2)}) copy-start(bf16[128,2048]{1,0:T(8,128)(2,1)} %all-reduce.12.cloned.1.call-done) | copy-start | bytes 1572868
  897.4 108.6 %copy-start.14 = (bf16[128,4,4,64]{0,3,2,1:T(8,128)(2,1)S(1)}, bf16[128,4,4,64]{0,3,2,1:T(8,128)(2,1)}, u32[]{:S(2)}) copy-start(bf16[128,4,4,64]{0,3,2,1:T(8,128)(2,1)} %copy-done.13) | copy-start | bytes 786436
  897.4 108.6 %copy-start.25 = (f32[16,1,128]{2,1,0:T(1,128)S(1)}, f32[16,1,128]{2,1,0:T(1,128)}, u32[]{:S(2)}) copy-start(f32[16,1,128]{2,1,0:T(1,128)} %copy-done.24) | copy-start | bytes 24580
  897.4 108.6 %copy-start.31 = (f32[128]{0:T(128)S(1)}, f32[128]{0:T(128)}, u32[]{:S(2)}) copy-start(f32[128]{0:T(128)} %copy-done.30) | copy-start | bytes 1540
  897.4 108.6 %copy-start.33 = (f32[128]{0:T(128)S(1)}, f32[128]{0:T(128)}, u32[]{:S(2)}) copy-start(f32[128]{0:T(128)} %copy-done.32) | copy-start | bytes 1540
  1006.1 4.8 copy-start.3
  1006.1 4.8 copy-start.12
  1010.9 13.5 copy-start.11
  1024.4 13.3 copy-start.18
  1024.4 13.3 copy-start.23
  1024.4 13.8 copy-start.17
  1024.4 14.3 copy-start.4
  1024.4 14.3 copy-start.16
  1041.1 2049.0 %all-reduce.14.cloned.1.call-start = ((), (), s32[]{:S(2)}) async-start(), calls=%async_computation.15 | async-start | bytes 243269632
  1054.8 0.7 copy-start.35
  1054.8 28.6 copy-start.27
Sparse Core Ops, SparseCore 0:
  10.2 40.4 all-gather.15
  52.8 36.8 all-gather.11
  92.5 36.8 all-gather.17
  131.9 36.8 all-gather.13
  170.8 49.4 all-gather.19
  222.3 49.0 all-gather.21
  276.1 26.6 all-reduce.9
  305.2 127.3 all-gather.25
  434.9 125.0 all-gather.23
  562.3 125.0 all-gather.27
  736.6 26.3 all-reduce.11
  877.6 59.9 reduce-scatter.2
  942.5 60.6 reduce-scatter.4
  1041.2 40.7 all-reduce.15
  1086.6 2003.3 all-reduce.13
where the time goes:
time: 3120 us; the launch traced here: 3110 us
  waiting for transfers between devices  2660 us (85%)
  matrix products  188 us (6%)
  local copies, waits for them, and re-layouts  120 us (4%)
  blocking collectives  102 us (3%)
    unnamed x16, waiting for transfers between devices  1950 us
    all_gather x1, waiting for transfers between devices, local(): slab_up = lax.all_gather(w_up, 'ctx', axis=0, tiled=True)  127 us
    all_gather x1, waiting for transfers between devices, local(): slab_gate = lax.all_gather(w_gate, 'ctx', axis=0, tiled=True)  118 us
    all_gather x1, waiting for transfers between devices, local(): lax.all_gather(w_down, 'ctx', axis=0, tiled=True)  118 us
    dynamic_update_slice x8, local copies, waits for them, and re-layouts, local(): lax.scan(grad_step, jnp.zeros((row_count, kv_heads, group_length, HEAD_DI...  79.4 us
  transfers between devices with their start and end apart: 15, of which 15 were waited for; matrix products, arithmetic and copies ran while one was open for 4% of the time, Pallas kernels for 0%

commit v1 on v0

v1 whole, which is shorter than its diff:
```python
import math

import jax
import jax.numpy as jnp
from jax import lax
from jax.experimental import pallas as pl
from jax.experimental.pallas import tpu as pltpu
from jax.sharding import Mesh
from jax.sharding import PartitionSpec as P

HEAD_DIM = 64
BLOCK = 64
EPS = 1e-05
THETA = 500000.0
NEG = -1e30
MESH = pl.DeviceIdType.MESH
AXES = ("yh", "z", "x", "core", "tp")
NN = (((1,), (0,)), ((), ()))
NT = (((1,), (1,)), ((), ()))
TN = (((0,), (0,)), ((), ()))
F32 = jnp.float32
BF16 = jnp.bfloat16
CHUNKS = 4
TMP = 256


def dot(a, b, dims):
    return lax.dot_general(a, b, dims, preferred_element_type=F32)


def mod(a, n):
    return lax.rem(a, jnp.int32(n))


class Sems:
    def __init__(self):
        self.size = 0

    def take(self, count):
        first = self.size
        self.size += count
        return first


class Plan:
    def __init__(self, sizes, model, heads_cols, kv_cols, hidden_cols, tokens):
        self.YH, self.Z, self.X, self.TP = sizes
        self.n_ctx = self.YH * self.Z * self.X * 2
        self.n_dev = self.n_ctx * self.TP
        self.S = self.YH * self.X * 2
        self.R = model // self.n_ctx
        self.model = model
        self.qc = heads_cols // self.Z
        self.kc = kv_cols // self.Z
        self.fc = hidden_cols // self.Z
        self.cols = [self.qc + 2 * self.kc, self.qc, self.fc, self.fc, self.fc]
        self.half = tokens // 2
        self.rows = 2 * self.Z * self.half
        self.seq = self.S * self.rows
        self.nseg = self.n_ctx // 2
        self.tile = 256 if self.seq <= 2048 else 128
        send, recv, local = Sems(), Sems(), Sems()
        W, Z, S, YX = 5, self.Z, self.S, self.YH * self.X
        self.gain_s, self.gain_r = send.take(self.n_ctx), recv.take(1)
        self.swap_s, self.swap_r = send.take(2), recv.take(2)
        self.s1_s, self.s1_r, self.s1_l = send.take(W * Z), recv.take(W * Z * 2), local.take(W)
        self.s2_s, self.s2_r = send.take(W * Z * S), recv.take(W * YX * Z)
        self.ag_s, self.ag_r = send.take(4 * 2 * Z), recv.take(4 * 2 * Z)
        self.rb_s, self.rb_r = send.take(4 * CHUNKS), recv.take(4 * CHUNKS)
        self.rz_s, self.rz_r = send.take(4 * CHUNKS * Z), recv.take(4 * CHUNKS * Z)
        self.kv_s, self.kv_r = send.take(S), recv.take(S)
        self.dkv_s, self.dkv_r = send.take(S), recv.take(S)
        self.dw_s, self.dw_r = send.take(W * self.nseg), recv.take(W * S * Z)
        self.og_s, self.og_r = send.take(W * Z * 2), recv.take(W * Z)
        self.og_l = local.take(W)
        self.out_s, self.out_r, self.out_l = send.take(4), recv.take(4), local.take(2)
        self.gg_s, self.gg_r = send.take(self.n_dev), recv.take(1)
        self.tmp_l = local.take(2 * S)
        self.n_send, self.n_recv, self.n_local = send.size, recv.size, local.size


def block_kernel(
    p,
    tok, cot, gin, cosr, sinr, posq, ids, wi0, wi1, wi2, wi3, wi4,
    block_out, in_grad, gain_grad, og0, og1, og2, og3, og4, rb0, rb1, rb2, rb3, rb4,
    gbuf, swap, n1, n2, gg, ga, w0, w1, w2, w3, w4, qpad, gmpad, kvall, kvt, dkv, lse, ot, gmt, mixed,
    hid, dgate, dup, dq, dkvr, gqkv, bsend, brecv, zsend, zrecv, resid, outv, ggs, ggr, tmp,
    ssem, rsem, lsem,
):
    YH, Z, X, S, R = p.YH, p.Z, p.X, p.S, p.R
    H = p.half
    HALF = Z * H
    win = [wi0, wi1, wi2, wi3, wi4]
    w = [w0, w1, w2, w3, w4]
    og = [og0, og1, og2, og3, og4]
    rb = [rb0, rb1, rb2, rb3, rb4]
    yh, z, x, c, tp = (lax.axis_index(a) for a in AXES)
    sib = {"core": 1 - c}
    holder = c == tp
    other = c != tp
    ctx_of = lambda a, b, d, e: ((a * Z + b) * X + d) * 2 + e
    ctx_me = ctx_of(yh, z, x, c)
    s_me = (yh * X + x) * 2 + tp
    zplus = lambda d: mod(z + d, Z)
    zminus = lambda d: mod(z + (Z - d), Z)
    row_of = lambda i, m: pl.multiple_of(i * m, m)

    def rc(src, dst, si, ri, dev):
        return pltpu.make_async_remote_copy(
            src_ref=src, dst_ref=dst, send_sem=ssem.at[si], recv_sem=rsem.at[ri],
            device_id=dev, device_id_type=MESH,
        )

    def wait_recv(dst, ri):
        rc(dst, dst, 0, ri, sib).wait_recv()

    def wait_send(src, si):
        rc(src, src, si, 0, sib).wait_send()

    def lc(src, dst, li):
        return pltpu.make_async_copy(src, dst, lsem.at[li])

    deltas = [
        (a, b, d, e, f)
        for a in range(YH) for b in range(Z) for d in range(X) for e in range(2) for f in range(p.TP)
        if a + b + d + e + f
    ]

    def away(a, b, d, e, f):
        return {
            "yh": mod(yh + a, YH), "z": mod(z + b, Z), "x": mod(x + d, X),
            "core": mod(c + e, 2), "tp": mod(tp + f, p.TP),
        }

    barrier = pltpu.get_barrier_semaphore()
    for delta in deltas:
        pl.semaphore_signal(barrier, inc=1, device_id=away(*delta), device_id_type=MESH)
    pl.semaphore_wait(barrier, len(deltas))

    gain_peers = [d for d in deltas if d[4] == 0]
    gbuf[ctx_me] = gin[...]
    for n, delta in enumerate(gain_peers):
        rc(gin, gbuf.at[ctx_me], p.gain_s + n, p.gain_r, away(*delta)).start()
    for n, src in enumerate((tok, cot)):
        rc(src.at[pl.ds(row_of(1 - c, H), H)], swap.at[n], p.swap_s + n, p.swap_r + n, sib).start()

    def seg(a, b, d):
        return pl.ds(pl.multiple_of(ctx_of(a, b, d, 0) * R, 2 * R), 2 * R)

    def block(a, b, d, e):
        return pl.ds(pl.multiple_of(ctx_of(a, b, d, e) * R, R), R)

    def piece(i, zz):
        if i == 0:
            return win[0].at[zz]
        n = p.cols[i]
        return win[i].at[:, pl.ds(pl.multiple_of(zz * n, n), n)]

    def w_stage1(i):
        dst = w[i].at[block(yh, z, x, c)]
        for d in range(Z):
            src = piece(i, zplus(d))
            si, ri = p.s1_s + i * Z + d, p.s1_r + (i * Z + d) * 2 + c
            if d == 0:
                @pl.when(holder)
                def _():
                    lc(src, dst, p.s1_l + i).start()

                @pl.when(other)
                def _():
                    rc(src, dst, si, ri, {"core": tp}).start()
            else:
                rc(src, dst, si, ri, {"z": zplus(d), "core": tp}).start()

    def w_stage1_sent(i):
        for d in range(Z):
            src = piece(i, zplus(d))
            if d == 0:
                @pl.when(other)
                def _():
                    wait_send(src, p.s1_s + i * Z + d)
            else:
                wait_send(src, p.s1_s + i * Z + d)

    plane = [(a, d, f) for a in range(YH) for d in range(X) for f in range(2) if a + d + f]

    def w_forward(i):
        @pl.when(holder)
        def _():
            for d in range(Z):
                zs = zminus(d)
                if d == 0:
                    lc(piece(i, z), w[i].at[block(yh, z, x, c)], p.s1_l + i).wait()
                    wait_recv(w[i].at[block(yh, z, x, 1 - c)], p.s1_r + i * Z * 2 + 1 - c)
                else:
                    for e in range(2):
                        wait_recv(w[i].at[block(yh, zs, x, e)], p.s1_r + (i * Z + d) * 2 + e)
                part = w[i].at[seg(yh, zs, x)]
                for n, (a, dx, f) in enumerate(plane):
                    rc(
                        part, part, p.s2_s + (i * Z + d) * S + n,
                        p.s2_r + (i * YH * X + a * X + dx) * Z + d, away(a, 0, dx, 0, f),
                    ).start()

    def w_wait(i):
        for a in range(YH):
            for dx in range(X):
                def wait_one():
                    for d in range(Z):
                        part = w[i].at[seg(mod(yh + YH - a, YH), zminus(d), mod(x + X - dx, X))]
                        wait_recv(part, p.s2_r + (i * YH * X + a * X + dx) * Z + d)
                if a + dx:
                    wait_one()
                else:
                    pl.when(other)(wait_one)

    def w_forward_sent(i):
        @pl.when(holder)
        def _():
            for d in range(Z):
                for n in range(len(plane)):
                    wait_send(w[i].at[seg(yh, zminus(d), x)], p.s2_s + (i * Z + d) * S + n)

    def rows_at(e, b):
        return pl.ds(pl.multiple_of((e * Z + b) * H, H), H)

    def ag_start(k, buf):
        mine = buf.at[rows_at(c, z)]
        base = k * 2 * Z
        for d in range(1, Z):
            rc(mine, mine, p.ag_s + base + d, p.ag_r + base + d, {"z": zplus(d)}).start()
        rc(mine, mine, p.ag_s + base, p.ag_r + base, sib).start()

    def ag_finish(k, buf):
        base = k * 2 * Z
        for d in range(1, Z):
            part = buf.at[rows_at(c, zminus(d))]
            wait_recv(part, p.ag_r + base + d)
            rc(part, part, p.ag_s + base + Z + d, p.ag_r + base + Z + d, sib).start()
        wait_recv(buf.at[rows_at(1 - c, z)], p.ag_r + base)
        for d in range(1, Z):
            wait_recv(buf.at[rows_at(1 - c, zminus(d))], p.ag_r + base + Z + d)

    def ag_sent(k, buf):
        base = k * 2 * Z
        for d in range(Z):
            wait_send(buf.at[rows_at(c, z)], p.ag_s + base + d)
        for d in range(1, Z):
            wait_send(buf.at[rows_at(c, zminus(d))], p.ag_s + base + Z + d)

    CW = p.model // CHUNKS

    def rs_start(k, terms):
        u = k % 2
        theirs = pl.ds(pl.multiple_of((1 - c) * HALF, HALF), HALF)
        own = pl.ds(pl.multiple_of(c * HALF, HALF), HALF)

        def product(j, rows):
            cols = pl.ds(pl.multiple_of(j * CW, CW), CW)
            total = None
            for a, b in terms:
                part = dot(a[rows, :], b[cols, :], NT)
                total = part if total is None else total + part
            return total

        def first(j, carry):
            value = product(j, theirs).astype(BF16)
            if k:
                wait_send(bsend.at[j], p.rb_s + (k - 1) * CHUNKS + j)
            bsend[j] = value
            rc(bsend.at[j], brecv.at[k, j], p.rb_s + k * CHUNKS + j, p.rb_r + k * CHUNKS + j, sib).start()
            return carry

        lax.fori_loop(0, CHUNKS, first, 0)

        def second(j, carry):
            value = product(j, own)
            wait_recv(brecv.at[k, j], p.rb_r + k * CHUNKS + j)
            zsend[u, j] = (value + brecv[k, j].astype(F32)).astype(BF16)
            for d in range(1, Z):
                ix = (k * CHUNKS + j) * Z + d
                rc(
                    zsend.at[u, j, pl.ds(row_of(zplus(d), H), H)], zrecv.at[k, j, d - 1],
                    p.rz_s + ix, p.rz_r + ix, {"z": zplus(d)},
                ).start()
            return carry

        lax.fori_loop(0, CHUNKS, second, 0)

    def rs_finish(k):
        u = k % 2
        parts = []
        for j in range(CHUNKS):
            value = zsend[u, j, pl.ds(row_of(z, H), H), :].astype(F32)
            for d in range(1, Z):
                wait_recv(zrecv.at[k, j, d - 1], p.rz_r + (k * CHUNKS + j) * Z + d)
                value = value + zrecv[k, j, d - 1].astype(F32)
            parts.append(value)
        return jnp.concatenate(parts, axis=1)

    def rs_sent(k):
        u = k % 2

        for j in range(CHUNKS):
            if k == 3:
                wait_send(bsend.at[j], p.rb_s + k * CHUNKS + j)
            for d in range(1, Z):
                wait_send(zsend.at[u, j, pl.ds(0, H)], p.rz_s + (k * CHUNKS + j) * Z + d)

    def dw_send(i, rows_ref, grad):
        per = 256 // (2 * R)

        def one(t, carry):
            cols = pl.ds(pl.multiple_of(t * 256, 256), 256)
            w[i][cols, :] = dot(rows_ref[:, cols], grad[...], TN).astype(BF16)
            for n in range(per):
                g = t * per + n
                xd, zd, yd = mod(g, X), mod(lax.div(g, jnp.int32(X)), Z), lax.div(g, jnp.int32(X * Z))
                mine = (xd == x) & (yd == yh) & holder

                @pl.when(jnp.logical_not(mine))
                def _():
                    rc(
                        w[i].at[pl.ds(pl.multiple_of(g * 2 * R, 2 * R), 2 * R)], rb[i].at[s_me, zd],
                        p.dw_s + i * p.nseg + g, p.dw_r + (i * S + s_me) * Z + zd,
                        {"yh": yd, "x": xd, "tp": c},
                    ).start()
            return carry

        lax.fori_loop(0, p.model // 256, one, 0)

    def dw_sent(i):
        for g in range(p.nseg):
            mine = (g % X == x) & (g // (X * Z) == yh) & holder

            @pl.when(jnp.logical_not(mine))
            def _():
                wait_send(w[i].at[pl.ds(g * 2 * R, 2 * R)], p.dw_s + i * p.nseg + g)

    def dw_reduce(i):
        n = p.cols[i]
        items = [(zd, at, min(TMP, n - at)) for zd in range(Z) for at in range(0, n, TMP)]

        def loads(q):
            zd, at, width = items[q]
            return [
                lc(
                    rb[i].at[mod(s_me + d, S), zd, :, pl.ds(at, width)],
                    tmp.at[q % 2, d - 1, :, pl.ds(0, width)], p.tmp_l + q % 2 * S + d,
                )
                for d in range(1, S)
            ]

        def begin(q):
            zd, at, _ = items[q]
            if at == 0:
                for d in range(1, S):
                    s = mod(s_me + d, S)
                    wait_recv(rb[i].at[s, zd], p.dw_r + (i * S + s) * Z + zd)
            for copy in loads(q):
                copy.start()

        @pl.when(holder)
        def _():
            begin(0)
            for q, (zd, at, width) in enumerate(items):
                if q + 1 < len(items):
                    begin(q + 1)
                for copy in loads(q):
                    copy.wait()
                mine = seg(yh, zd, x)
                total = w[i][mine, at : at + width].astype(F32)
                for d in range(1, S):
                    total = total + tmp[q % 2, d - 1, :, 0:width].astype(F32)
                w[i][mine, at : at + width] = total.astype(BF16)
                if at + width < n:
                    continue
                for e in range(2):
                    src = w[i].at[block(yh, zd, x, e)]
                    here = (z == zd) & (c == e)

                    @pl.when(here)
                    def _():
                        lc(src, og[i].at[z], p.og_l + i).start()

                    @pl.when(jnp.logical_not(here))
                    def _():
                        rc(
                            src, og[i].at[z], p.og_s + (i * Z + zd) * 2 + e, p.og_r + i * Z + z,
                            {"z": jnp.int32(zd), "core": jnp.int32(e)},
                        ).start()

    def dw_done(i):
        for b in range(Z):
            here = (z == b) & holder

            @pl.when(here)
            def _():
                lc(w[i].at[block(yh, z, x, c)], og[i].at[z], p.og_l + i).wait()

            @pl.when(jnp.logical_not(here))
            def _():
                wait_recv(og[i].at[b], p.og_r + i * Z + b)

        @pl.when(holder)
        def _():
            for zd in range(Z):
                for e in range(2):
                    @pl.when(jnp.logical_not((z == zd) & (c == e)))
                    def _():
                        wait_send(w[i].at[block(yh, zd, x, e)], p.og_s + (i * Z + zd) * 2 + e)

    def deliver(k, out):
        dst = out.at[pl.ds(row_of(c, H), H)]
        for t in range(p.TP):
            here = holder & (tp == t)

            @pl.when(here)
            def _():
                lc(outv.at[k], dst, p.out_l + k).start()

            @pl.when(jnp.logical_not(here))
            def _():
                rc(outv.at[k], dst, p.out_s + k * 2 + t, p.out_r + k * 2 + c, {"core": tp, "tp": jnp.int32(t)}).start()

    def delivered(k, out):
        for e in range(2):
            here = holder & (c == e)

            @pl.when(here)
            def _():
                lc(outv.at[k], out.at[pl.ds(row_of(c, H), H)], p.out_l + k).wait()

            @pl.when(jnp.logical_not(here))
            def _():
                wait_recv(out.at[pl.ds(e * H, H)], p.out_r + k * 2 + e)
        for t in range(p.TP):
            @pl.when(jnp.logical_not(holder & (tp == t)))
            def _():
                wait_send(outv.at[k], p.out_s + k * 2 + t)

    w_stage1(0)
    for n in range(2):
        wait_recv(swap.at[n], p.swap_r + n)
    mine = pl.ds(row_of(c, H), H)
    token_rows = jnp.where(holder, tok[mine, :].astype(F32), swap[0].astype(F32))
    grad_rows = jnp.where(holder, cot[mine, :].astype(F32), swap[1].astype(F32))
    gg[rows_at(c, z), :] = grad_rows.astype(BF16)
    factor_attn = lax.rsqrt(jnp.mean(token_rows * token_rows, axis=1, keepdims=True) + EPS)
    scaled_attn = token_rows * factor_attn
    wait_recv(gbuf.at[pl.ds(0, p.n_ctx - 1)], p.gain_r)
    q = p.n_ctx * 128 // p.model
    gain_parts = []
    for b in range(p.model // 128):
        total = gbuf[b * q]
        for n in range(1, q):
            total = total + gbuf[b * q + n]
        gain_parts.append(total)
    gains = jnp.concatenate(gain_parts, axis=1)
    gain_attn, gain_mlp = gains[0:1, :], gains[1:2, :]
    n1[rows_at(c, z), :] = (scaled_attn * gain_attn).astype(BF16)
    ag_start(0, n1)
    w_forward(0)
    w_stage1(1)
    ag_finish(0, n1)
    ag_start(1, gg)
    for i in (2, 3, 4):
        w_stage1(i)
    w_wait(0)

    lane = lax.broadcasted_iota(jnp.int32, (1, 128), 1)
    low = lane < HEAD_DIM
    first_half = mod(lane, HEAD_DIM) < HEAD_DIM // 2

    def rotate(t, cosine, sine):
        turned = jnp.where(first_half, pltpu.roll(t, 96, 1), pltpu.roll(t, 32, 1))
        return t * cosine + turned * sine

    lin = dot(n1[...], w0[...], NN)
    cosine, sine = cosr[...], sinr[...]
    scale = HEAD_DIM ** (-0.5)
    pairs = p.qc // 128
    for n in range(pairs):
        turned_q = rotate(lin[:, n * 128 : (n + 1) * 128], cosine, sine).astype(BF16).astype(F32) * scale
        qpad[2 * n] = jnp.where(low, turned_q, 0.0).astype(BF16)
        qpad[2 * n + 1] = jnp.where(low, pltpu.roll(turned_q, 64, 1), 0.0).astype(BF16)
    kv_lin = lin[:, p.qc : p.qc + 128]
    own_rows = pl.ds(pl.multiple_of(s_me * p.rows, p.rows), p.rows)
    kvall[own_rows, :] = jnp.where(low, rotate(kv_lin, cosine, sine), kv_lin).astype(BF16)
    for n, (a, dx, f) in enumerate(plane):
        rc(kvall.at[own_rows], kvall.at[own_rows], p.kv_s + n, p.kv_r + n, away(a, 0, dx, 0, f)).start()

    def from_plane(a, dx, f):
        s = (mod(yh + YH - a, YH) * X + mod(x + X - dx, X)) * 2 + mod(tp + 2 - f, 2)
        return pl.ds(pl.multiple_of(s * p.rows, p.rows), p.rows)

    for n, delta in enumerate(plane):
        wait_recv(kvall.at[from_plane(*delta)], p.kv_r + n)
    eye = (
        lax.broadcasted_iota(jnp.int32, (128, 128), 0) == lax.broadcasted_iota(jnp.int32, (128, 128), 1)
    ).astype(BF16)
    kvt[...] = dot(eye, kvall[...], NT).astype(BF16)

    T = p.tile
    KC = p.rows
    down = lax.broadcasted_iota(jnp.int32, (BLOCK, 1), 0)

    def masked(s, rows, scores):
        at = posq[:, rows]
        parts = []
        for b in range(2 * Z):
            allowed = down <= at - ids[s, b] * BLOCK
            parts.append(jnp.where(allowed, scores[b * BLOCK : (b + 1) * BLOCK, :], NEG))
        return jnp.concatenate(parts, axis=0)

    def keys(s):
        return pl.ds(s * KC, KC)

    for n in range(pairs):
        def attend(t, carry):
            rows = pl.ds(pl.multiple_of(t * T, T), T)
            outs = []
            for e in range(2):
                h = 2 * n + e
                query = qpad[h, rows, :]
                top = jnp.full((8, T), NEG, F32)
                for s in range(S):
                    scores = masked(s, rows, dot(kvall[keys(s), :], query, NT))
                    dkv[keys(s), :] = scores
                    top = jnp.maximum(top, jnp.max(scores.reshape(KC // 8, 8, T), axis=0))
                top = jnp.max(top, axis=0, keepdims=True)
                total = jnp.zeros((8, T), F32)
                for s in range(S):
                    grown = jnp.exp(dkv[keys(s), :] - top)
                    dkv[keys(s), :] = grown
                    total = total + jnp.sum(grown.reshape(KC // 8, 8, T), axis=0)
                total = jnp.sum(total, axis=0, keepdims=True)
                lse[h : h + 1, rows] = top + jnp.log(total)
                share = 1.0 / total
                out = jnp.zeros((128, T), F32)
                for s in range(S):
                    out = out + dot(kvt[:, keys(s)], (dkv[keys(s), :] * share).astype(BF16), NN)
                outs.append(out[HEAD_DIM:, :])
            out = jnp.concatenate(outs, axis=0)
            ot[n, :, rows] = out
            mixed[rows, n * 128 : (n + 1) * 128] = jnp.transpose(out).astype(BF16)
            return carry

        lax.fori_loop(0, p.rows // T, attend, 0)
        if n == 0:
            w_forward(1)
            w_forward(2)
    w_forward(3)
    w_forward(4)
    w_wait(1)
    rs_start(0, [(mixed, w1)])
    ag_finish(1, gg)
    residual = token_rows + rs_finish(0)
    resid[...] = residual
    factor_mlp = lax.rsqrt(jnp.mean(residual * residual, axis=1, keepdims=True) + EPS)
    scaled_mlp = residual * factor_mlp
    n2[rows_at(c, z), :] = (scaled_mlp * gain_mlp).astype(BF16)
    ag_start(2, n2)
    for i in (2, 3, 4):
        w_wait(i)
    ag_finish(2, n2)

    def feed(t, carry):
        cols = pl.ds(pl.multiple_of(t * 256, 256), 256)
        gate = dot(n2[...], w2[:, cols], NN)
        up = dot(n2[...], w3[:, cols], NN)
        back = dot(gg[...], w4[:, cols], NN)
        sig = jax.nn.sigmoid(gate)
        silu = gate * sig
        hid[:, cols] = (silu * up).astype(BF16)
        dgate[:, cols] = (back * up * sig * (1.0 + gate * (1.0 - sig))).astype(BF16)
        dup[:, cols] = (back * silu).astype(BF16)
        return carry

    lax.fori_loop(0, p.fc // 256, feed, 0)
    rs_start(1, [(dgate, w2), (dup, w3)])
    rs_sent(0)
    rs_start(2, [(hid, w4)])
    w_forward_sent(4)
    dw_send(4, gg, hid)
    grad_norm_mlp = rs_finish(1)
    weighted = grad_norm_mlp * gain_mlp
    u = resid[...] * factor_mlp
    grad_residual = grad_rows + factor_mlp * (weighted - u * jnp.mean(weighted * u, axis=1, keepdims=True))
    gain_mlp_part = jnp.sum(grad_norm_mlp * u, axis=0, keepdims=True)
    ga[rows_at(c, z), :] = grad_residual.astype(BF16)
    ag_start(3, ga)
    w_forward_sent(2)
    dw_send(2, n2, dgate)
    w_forward_sent(3)
    dw_send(3, n2, dup)
    outv[0] = (resid[...] + rs_finish(2)).astype(BF16)
    resid[...] = grad_residual
    deliver(0, block_out)
    ag_finish(3, ga)

    for n in range(pairs):
        gm = dot(ga[...], w1[:, n * 128 : (n + 1) * 128], NN).astype(BF16).astype(F32)
        gmt[n] = jnp.transpose(gm)
        gmpad[2 * n] = jnp.where(low, 0.0, pltpu.roll(gm, 64, 1)).astype(BF16)
        gmpad[2 * n + 1] = jnp.where(low, 0.0, gm).astype(BF16)
    w_forward_sent(1)
    dw_send(1, ga, mixed)
    dkv[:, 0:128] = jnp.zeros((p.seq, 128), F32)
    for n in range(pairs):
        def attend_back(t, carry):
            rows = pl.ds(pl.multiple_of(t * T, T), T)
            agree = ot[n, :, rows] * gmt[n, :, rows]
            outs = []
            for e in range(2):
                h = 2 * n + e
                query, back = qpad[h, rows, :], gmpad[h, rows, :]
                level = lse[h : h + 1, rows]
                delta = jnp.sum(agree[e * HEAD_DIM : (e + 1) * HEAD_DIM, :], axis=0, keepdims=True)
                out = jnp.zeros((128, T), F32)
                for s in range(S):
                    here = kvall[keys(s), :]
                    probs = jnp.exp(masked(s, rows, dot(here, query, NT)) - level)
                    ds = (probs * (dot(here, back, NT) - delta)).astype(BF16)
                    out = out + dot(kvt[:, keys(s)], ds, NN)
                    dkv[keys(s), 0:128] += dot(ds, query, NN) + dot(probs.astype(BF16), back, NN)
                outs.append(out[:HEAD_DIM, :])
            dq[rows, n * 128 : (n + 1) * 128] = jnp.transpose(jnp.concatenate(outs, axis=0)) * scale
            return carry

        lax.fori_loop(0, p.rows // T, attend_back, 0)
    for n, (a, dx, f) in enumerate(plane):
        s = (mod(yh + a, YH) * X + mod(x + dx, X)) * 2 + mod(tp + f, 2)
        rc(
            dkv.at[pl.ds(pl.multiple_of(s * p.rows, p.rows), p.rows), pl.ds(0, 128)], dkvr.at[n],
            p.dkv_s + n, p.dkv_r + n, away(a, 0, dx, 0, f),
        ).start()
    for n in range(pairs):
        cols = slice(n * 128, (n + 1) * 128)
        gqkv[:, cols] = rotate(dq[:, cols], cosine, -sine).astype(BF16)
    dw_reduce(4)
    dw_reduce(2)
    dkv_own = dkv[own_rows, 0:128]
    for n in range(len(plane)):
        wait_recv(dkvr.at[n], p.dkv_r + n)
        dkv_own = dkv_own + dkvr[n]
    gqkv[:, p.qc : p.qc + 128] = jnp.where(low, rotate(dkv_own, cosine, -sine), dkv_own).astype(BF16)
    rs_sent(1)
    rs_start(3, [(gqkv, w0)])
    w_forward_sent(0)
    dw_send(0, n1, gqkv)
    dw_reduce(3)
    dw_reduce(1)
    grad_norm_attn = rs_finish(3)
    weighted = grad_norm_attn * gain_attn
    outv[1] = (
        resid[...] + factor_attn * (weighted - scaled_attn * jnp.mean(weighted * scaled_attn, axis=1, keepdims=True))
    ).astype(BF16)
    deliver(1, in_grad)

    gain_attn_part = jnp.sum(grad_norm_attn * scaled_attn, axis=0, keepdims=True)
    both_gains = jnp.concatenate([gain_attn_part, gain_mlp_part, jnp.zeros((6, p.model), F32)], axis=0)
    for b in range(p.model // 128):
        ggs[b] = both_gains[:, b * 128 : (b + 1) * 128]
    dev_me = ctx_me * p.TP + tp
    ggr[dev_me] = ggs[lax.div(ctx_me * R, jnp.int32(128))]
    for n, delta in enumerate(deltas):
        to = away(*delta)
        there = ctx_of(to["yh"], to["z"], to["x"], to["core"])
        rc(ggs.at[lax.div(there * R, jnp.int32(128))], ggr.at[dev_me], p.gg_s + n, p.gg_r, to).start()

    dw_reduce(0)
    wait_recv(ggr.at[pl.ds(0, p.n_dev - 1)], p.gg_r)
    total = ggr[0]
    for n in range(1, p.n_dev):
        total = total + ggr[n]
    gain_grad[...] = total

    for i in range(5):
        dw_done(i)
        dw_sent(i)
        w_stage1_sent(i)
    for k, buf in enumerate((n1, gg, n2, ga)):
        ag_sent(k, buf)
    rs_sent(2)
    rs_sent(3)
    delivered(0, block_out)
    delivered(1, in_grad)
    for n in range(len(plane)):
        wait_send(kvall.at[own_rows], p.kv_s + n)
        wait_send(dkvr.at[n], p.dkv_s + n)
    for n in range(len(gain_peers)):
        wait_send(gin, p.gain_s + n)
    for n in range(len(deltas)):
        wait_send(ggs.at[0], p.gg_s + n)
    for n in range(2):
        wait_send(swap.at[n], p.swap_s + n)


def local(sizes, tokens, block_ids, gain_attn, w_query, key_weight, value_weight, w_out, gain_mlp,
          w_gate, w_up, w_down, cotangent):
    row_count, model = tokens.shape
    p = Plan(sizes, model, w_query.shape[1], key_weight.shape[1], w_gate.shape[1], row_count)
    YH, Z, X, S, R = p.YH, p.Z, p.X, p.S, p.R
    yh, z, x, c, tp = (lax.axis_index(a) for a in AXES)
    ctx_me = ((yh * Z + z) * X + x) * 2 + c
    s_me = (yh * X + x) * 2 + tp
    ids = block_ids.reshape(YH, Z, X, 2, 2).transpose(0, 2, 3, 4, 1).reshape(S, 2 * Z)
    positions = (ids[:, :, None] * BLOCK + jnp.arange(BLOCK, dtype=jnp.int32)).reshape(S, p.rows)
    own = lax.dynamic_slice_in_dim(positions, s_me, 1, 0)
    half = HEAD_DIM // 2
    frequencies = THETA ** (-(jnp.arange(half, dtype=F32) * 2.0 / HEAD_DIM))
    angles = own.reshape(p.rows, 1).astype(F32) * jnp.tile(frequencies, 4)[None, :]
    signs = jnp.where(jnp.arange(128) % HEAD_DIM < half, -1.0, 1.0).astype(F32)
    cosine, sine = jnp.cos(angles), jnp.sin(angles) * signs
    gains = jnp.stack([gain_attn, gain_mlp]).astype(F32)
    gin = lax.dynamic_update_slice(jnp.zeros((8, 128), F32), gains, (0, lax.rem(ctx_me * R, 128)))
    packed = jnp.concatenate(
        [w_query.reshape(R, Z, p.qc), key_weight.reshape(R, Z, p.kc), value_weight.reshape(R, Z, p.kc)], axis=2
    ).transpose(1, 0, 2)

    V = pl.BlockSpec(memory_space=pltpu.VMEM)
    A = pl.BlockSpec(memory_space=pl.ANY)
    H = p.half
    sd = jax.ShapeDtypeStruct
    out_shape = [sd((row_count, model), BF16), sd((row_count, model), BF16), sd((8, 128), F32)]
    out_shape += [sd((Z, R, n), BF16) for n in p.cols]
    out_shape += [sd((S, Z, 2 * R, n), BF16) for n in p.cols]
    CW = model // CHUNKS
    scratch = [
        pltpu.VMEM((p.n_ctx, 8, 128), F32),
        pltpu.VMEM((2, H, model), BF16),
        *[pltpu.VMEM((p.rows, model), BF16) for _ in range(4)],
        *[pltpu.VMEM((model, n), BF16) for n in p.cols],
        pltpu.VMEM((p.qc // 64, p.rows, 128), BF16),
        pltpu.VMEM((p.qc // 64, p.rows, 128), BF16),
        pltpu.VMEM((p.seq, 128), BF16),
        pltpu.VMEM((128, p.seq), BF16),
        pltpu.VMEM((p.seq, p.tile), F32),
        pltpu.VMEM((8, p.rows), F32),
        pltpu.VMEM((p.qc // 128, 128, p.rows), F32),
        pltpu.VMEM((p.qc // 128, 128, p.rows), F32),
        pltpu.VMEM((p.rows, p.qc), BF16),
        *[pltpu.VMEM((p.rows, p.fc), BF16) for _ in range(3)],
        pltpu.VMEM((p.rows, p.qc), F32),
        pltpu.VMEM((S - 1, p.rows, 128), F32),
        pltpu.VMEM((p.rows, p.cols[0]), BF16),
        pltpu.VMEM((CHUNKS, Z * H, CW), BF16),
        pltpu.VMEM((4, CHUNKS, Z * H, CW), BF16),
        pltpu.VMEM((2, CHUNKS, Z * H, CW), BF16),
        pltpu.VMEM((4, CHUNKS, Z - 1, H, CW), BF16),
        pltpu.VMEM((H, model), F32),
        pltpu.VMEM((2, H, model), BF16),
        pltpu.VMEM((model // 128, 8, 128), F32),
        pltpu.VMEM((p.n_dev, 8, 128), F32),
        pltpu.VMEM((2, S - 1, 2 * R, TMP), BF16),
        pltpu.SemaphoreType.DMA((p.n_send,)),
        pltpu.SemaphoreType.DMA((p.n_recv,)),
        pltpu.SemaphoreType.DMA((p.n_local,)),
    ]
    outs = pl.pallas_call(
        lambda *refs: block_kernel(p, *refs),
        out_shape=out_shape,
        in_specs=[V] * 6 + [pl.BlockSpec(memory_space=pltpu.SMEM)] + [A] * 5,
        out_specs=[A, A, V] + [A] * 10,
        scratch_shapes=scratch,
        compiler_params=pltpu.CompilerParams(
            collective_id=0, has_side_effects=True, vmem_limit_bytes=64000 * 1024
        ),
        name="block",
    )(
        tokens, cotangent, gin, cosine, sine, own, ids,
        packed, w_out, w_gate, w_up, w_down,
    )
    block_out, in_grad, gain_grad = outs[:3]
    g_qkv, g_out, g_gate, g_up, g_down = (
        g.transpose(1, 0, 2).astype(F32) for g in outs[3:8]
    )
    gain_grads = lax.dynamic_slice(gain_grad, (0, lax.rem(ctx_me * R, 128)), (2, R))
    return (
        block_out,
        in_grad,
        gain_grads[0],
        g_qkv[:, :, : p.qc].reshape(R, -1),
        g_qkv[:, :, p.qc : p.qc + p.kc].reshape(R, -1),
        g_qkv[:, :, p.qc + p.kc :].reshape(R, -1),
        g_out.reshape(R, -1),
        gain_grads[1],
        g_gate.reshape(R, -1),
        g_up.reshape(R, -1),
        g_down.reshape(R, -1),
    )


def solution(mesh):
    n_ctx, tp = mesh.devices.shape
    Z = 4
    X = 2 if n_ctx == 16 else 4
    YH = n_ctx // (Z * X * 2)
    sizes = (YH, Z, X, tp)
    split = Mesh(mesh.devices.reshape(YH, Z, X, 2, tp), AXES)
    ctx = AXES[:4]
    rows, weight, vector = P(ctx, None), P(ctx, "tp"), P(ctx)
    return jax.shard_map(
        lambda *args: local(sizes, *args),
        mesh=split,
        in_specs=(rows, P(), vector, weight, weight, weight, weight, vector, weight, weight, weight, rows),
        out_specs=(rows, rows, vector, weight, weight, weight, weight, vector, weight, weight, weight),
        check_vma=False,
    )
```

time: 3120 us -> 521 us (0.17)
  waiting for transfers between devices: 2660 us -> 0 us
  Pallas kernels: 0 us -> 482 us
  matrix products: 188 us -> 0 us
  blocking collectives: 102 us -> 0 us
  local copies, waits for them, and re-layouts: 120 us -> 27.2 us
    unnamed x16 -> x0, waiting for transfers between devices: 1950 us -> none
    all_gather x9 -> x0, waiting for transfers between devices: 558 us -> none  [the longest x1 127 us: local(): slab_up = lax.all_gather(w_up, 'ctx', axis=0, tiled=True)]
    pallas_call x0 -> x1, Pallas kernels: none -> 482 us  [local(): pl.pallas_call(lambda *refs: block_kernel(p, *refs), out_shape=out_shape,...]
    dot_general x35 -> x0, matrix products: 188 us -> none  [the longest x1 24 us: local(): jnp.einsum('rf,df->rd', grad_gate, slab_gate, preferred_element_type=jnp....]
    reduce_scatter x2 -> x0, waiting for transfers between devices: 97.2 us -> none  [the longest x1 61.6 us: local(): lax.psum_scatter(grad_value_blocks.reshape(sequence_length, kv_cols), 'ct...]
    dynamic_update_slice x8 -> x0, local copies, waits for them, and re-layouts: 79.4 us -> none  [local(): lax.scan(grad_step, jnp.zeros((row_count, kv_heads, group_length, HEAD_DI...]
    unnamed x1 -> x0, blocking collectives: 59.7 us -> none
    psum x3 -> x0, waiting for transfers between devices: 57.3 us -> none  [the longest x1 26.4 us: local(): lax.psum(grad_norm_part.astype(jnp.bfloat16), 'tp').astype(jnp.float32)]
  transfers between devices with their start and end apart: 15 -> 0, of which waited for: 15 -> 0; matrix products, arithmetic and copies ran while one was open for 4% -> 0% of each run, Pallas kernels for 0% -> 0%
where the time goes in v1:
time: 521 us; the launch traced here: 519 us
  Pallas kernels  482 us (93%)
  local copies, waits for them, and re-layouts  27.2 us (5%)
  other arithmetic  8.8 us (2%)
    pallas_call x1, Pallas kernels, local(): pl.pallas_call(lambda *refs: block_kernel(p, *refs), out_shape=out_shape,...  482 us
    unnamed x24, local copies, waits for them, and re-layouts  17 us

profile of v1, /device:TPU:1, one launch (start us, length us, event | category | flops | bytes accessed | tf_op | source)
XLA Modules:
  0.0 519.2 jit_solution(9268323534431795896)
XLA Ops:
  0.7 0.1 mul.50
  0.8 1.3 fusion.4.refs_2_
  2.0 0.1 add.47
  2.1 0.7 reshape.105
  2.9 0.1 copy.24
  3.0 0.1 broadcast_in_dim_reshape.3.refs_6_
  3.1 0.0 copy-start.5
  3.1 0.1 add.44
  3.1 0.1 add.45
  3.2 0.6 fusion.5
  3.8 0.9 copy.26
  4.8 0.1 copy.29
  4.9 1.0 copy.27
  5.9 0.1 copy.30
  6.0 1.1 copy.25
  7.1 0.1 copy.28
  7.3 0.9 maximum_bitcast_fusion.refs_7_
  8.2 1.8 fusion
  10.0 0.0 copy-done.5
  10.0 482.4 %block.1 = (bf16[128,2048]{1,0:T(8,128)(2,1)}, bf16[128,2048]{1,0:T(8,128)(2,1)}, f32[8,128]{1,0:T(8,128)}, bf16[4,128,384]{2,1,0:T(8,128)(2,1)}, bf16[4,128,256...) custom-call(bf16[128,2048]{1,0:T(8,128)(2,1)} %refs_0_.1, ...), custom_call_target="tpu_custom_call" | custom-call | tf_op jit(solution)/shard_map/block/pallas_call | solution.py:761
  492.4 0.0 copy-start.4
  492.4 1.3 slice_bitcast_fusion
  493.6 1.0 convert_bitcast_fusion.4
  494.6 0.2 copy.34
  494.8 1.0 copy.41
  495.8 0.0 copy-done.4
  495.8 0.1 convert_bitcast_fusion.3
  495.9 0.0 copy-start
  495.9 0.1 fusion.6
  496.1 0.1 copy.33
  496.2 0.8 copy.40
  497.0 0.2 copy.31
  497.2 1.0 copy.38
  498.2 0.1 copy.32
  498.3 0.8 copy.39
  499.0 0.0 copy-done
  499.0 0.2 convert_bitcast_fusion.2
  499.3 1.8 copy.35
  501.1 0.0 copy-start.1
  501.1 3.0 copy.42
  504.1 0.0 copy-done.1
  504.1 3.0 convert_bitcast_fusion
  507.0 2.9 copy.37
  509.9 2.9 copy.44
  512.8 1.8 copy.36
  514.6 0.0 copy-start.3
  514.6 0.0 copy-start.2
  514.6 3.0 copy.43
  517.6 0.0 copy-done.3
  517.6 0.8 copy.47
  518.4 0.0 copy-done.2
  518.4 0.8 copy.48
  (6 shorter events, 0.1 us)
Async XLA Ops:
  3.1 6.9 %copy-start.5 = (s32[4,8]{1,0:T(4,128)}, s32[4,8]{1,0:T(4,128)S(1)}, u32[]{:S(2)}) copy-start(s32[4,8]{1,0:T(4,128)S(1)} %broadcast_in_dim_reshape.3.refs_6_) | copy-start | bytes 388
  492.4 3.5 copy-start.4
  495.9 3.1 copy-start
  501.1 3.0 copy-start.1
  514.6 3.0 copy-start.3
  514.6 3.8 copy-start.2

commit v2 on v1

v2 whole, which is shorter than its diff:
```python
import math

import jax
import jax.numpy as jnp
from jax import lax
from jax.experimental import pallas as pl
from jax.experimental.pallas import tpu as pltpu
from jax.sharding import Mesh
from jax.sharding import PartitionSpec as P

HEAD_DIM = 64
BLOCK = 64
EPS = 1e-05
THETA = 500000.0
NEG = -1e30
MESH = pl.DeviceIdType.MESH
AXES = ("yh", "z", "x", "core", "tp")
NN = (((1,), (0,)), ((), ()))
NT = (((1,), (1,)), ((), ()))
TN = (((0,), (0,)), ((), ()))
F32 = jnp.float32
BF16 = jnp.bfloat16
CHUNKS = 4
TMP = 128
WIDE = (2, 3, 4)
ALL = (0, 1, 2, 3)
FILL = {
    "inputs": [("stage", 1, ALL)],
    "n1_0": [("stage", 2, ALL)],
    "n1_3": [("cotangent", 0), ("stage", 3, ALL)],
    "kv": [("forward", 1, ALL)],
    "attend_0": [("cotangent", 1)],
    "attend_1": [("cotangent", 2), ("forward", 2, ALL), ("stage", 4, ALL)],
    "attend_2": [("cotangent", 3), ("forward", 3, ALL)],
    "n2_2": [("forward", 4, ALL)],
    "norm_0": [("reduce", 4, (0,))],
    "norm_1": [("reduce", 4, (1,))],
    "norm_2": [("reduce", 4, (2,))],
    "norm_3": [("reduce", 4, (3,))],
    "ga_0": [("sum", (0, 1))],
    "ga_1": [("sum", (2, 3))],
    "ga_3": [("reduce", 2, (0, 1))],
    "back_0": [("reduce", 2, (2, 3))],
    "back_1": [("reduce", 3, (0, 1))],
    "back_2": [("reduce", 3, (2, 3))],
    "terms": [("reduce", 1, ALL)],
    "end_1": [("reduce", 0, ALL)],
}


def dot(a, b, dims):
    return lax.dot_general(a, b, dims, preferred_element_type=F32)


def mod(a, n):
    return lax.rem(a, jnp.int32(n))


class Sems:
    def __init__(self):
        self.size = 0

    def take(self, count):
        first = self.size
        self.size += count
        return first


class Plan:
    def __init__(self, sizes, model, heads_cols, kv_cols, hidden_cols, tokens):
        self.YH, self.Z, self.X, self.TP = sizes
        self.n_ctx = self.YH * self.Z * self.X * 2
        self.n_dev = self.n_ctx * self.TP
        self.S = self.YH * self.X * 2
        self.YX = self.YH * self.X
        self.R = model // self.n_ctx
        self.model = model
        self.qc = heads_cols // self.Z
        self.kc = kv_cols // self.Z
        self.fc = hidden_cols // (2 * self.Z)
        self.cols = [self.qc + 2 * self.kc, self.qc, self.fc, self.fc, self.fc]
        self.half = tokens // 2
        self.rows = 2 * self.Z * self.half
        self.wide_rows = 2 * self.rows
        self.seq = self.S * self.rows
        self.nseg = self.n_ctx // 2
        self.tile = 256 if self.seq <= 2048 else 128
        send, recv, local = Sems(), Sems(), Sems()
        W, Z, S, YX = 5, self.Z, self.S, self.YX
        self.gain_s, self.gain_r = send.take(self.n_ctx), recv.take(1)
        self.swap_s, self.swap_r = send.take(2), recv.take(2)
        self.s1_s, self.s1_r, self.s1_l = send.take(W * Z * 2), recv.take(W * Z * 2), local.take(W)
        self.s2_s, self.s2_r = send.take(W * Z * S), recv.take(W * YX * Z)
        self.ag_s, self.ag_r = send.take(4 * 5 * Z), recv.take(4 * 4 * Z)
        self.rb_s, self.rb_r = send.take(4 * CHUNKS), recv.take(4 * CHUNKS)
        self.ry_s, self.ry_r = send.take(4 * CHUNKS), recv.take(4 * CHUNKS)
        self.rz_s, self.rz_r = send.take(4 * CHUNKS * Z), recv.take(4 * CHUNKS * (Z + 1))
        self.kv_s, self.kv_r = send.take(S), recv.take(S)
        self.dkv_s, self.dkv_r = send.take(S), recv.take(S)
        self.dw_s, self.dw_r = send.take(W * self.nseg), recv.take(W * S * Z)
        self.og_s, self.og_r = send.take(W * Z * 2), recv.take(W * Z * 2)
        self.og_l = local.take(W)
        self.out_s, self.out_r, self.out_l = send.take(4), recv.take(4), local.take(2)
        self.gg_s, self.gg_r = send.take(self.n_dev), recv.take(1)
        self.tmp_l = local.take(2 * S)
        self.pack_l = local.take(3)
        self.n_send, self.n_recv, self.n_local = send.size, recv.size, local.size


def block_kernel(
    p,
    tok, cot, gin, cosr, sinr, posq, ids, wq, wk, wv, wi1, wi2, wi3, wi4,
    block_out, in_grad, gain_grad, og0, og1, og2, og3, og4, rb0, rb1, rb2, rb3, rb4,
    gbuf, swap, stq, stk, stv, pack, n1, n2, gg, ga, w0, w1, w2, w3, w4,
    qpad, gmpad, kvall, dkv, lse, ot, mixed, hid, dgate, dup, gate, up, dq, dkvr, gqkv,
    bsend, brecvs, ysend, yrecv, zsend, zrecv, acc, toks, resid, resid2, ggs, ggr, tmp,
    ssem, rsem, lsem,
):
    YH, Z, X, S, YX, R = p.YH, p.Z, p.X, p.S, p.YX, p.R
    H = p.half
    HALF = Z * H
    win = [None, wi1, wi2, wi3, wi4]
    w = [w0, w1, w2, w3, w4]
    og = [og0, og1, og2, og3, og4]
    rb = [rb0, rb1, rb2, rb3, rb4]
    yh, z, x, c, tp = (lax.axis_index(a) for a in AXES)
    sib = {"core": 1 - c}
    holder = c == tp
    other = c != tp
    ctx_of = lambda a, b, d, e: ((a * Z + b) * X + d) * 2 + e
    ctx_me = ctx_of(yh, z, x, c)
    s_me = (yh * X + x) * 2 + tp
    yx_me = yh * X + x
    zplus = lambda d: mod(z + d, Z)
    zminus = lambda d: mod(z + (Z - d), Z)
    row_of = lambda i, m: pl.multiple_of(i * m, m)
    pending = []

    def rc(src, dst, si, ri, dev):
        return pltpu.make_async_remote_copy(
            src_ref=src, dst_ref=dst, send_sem=ssem.at[si], recv_sem=rsem.at[ri],
            device_id=dev, device_id_type=MESH,
        )

    def wait_recv(dst, ri):
        rc(dst, dst, 0, ri, sib).wait_recv()

    def wait_send(src, si):
        rc(src, src, si, 0, sib).wait_send()

    def lc(src, dst, li):
        return pltpu.make_async_copy(src, dst, lsem.at[li])

    def when(pred, do):
        if pred is None:
            do()
        else:
            pl.when(pred)(do)

    def send(src, dst, si, ri, dev, pred=None):
        when(pred, lambda: rc(src, dst, si, ri, dev).start())
        pending.append(lambda: when(pred, lambda: wait_send(src, si)))

    loads = [lc(a, b, p.pack_l + n) for n, (a, b) in enumerate(((wq, stq), (wk, stk), (wv, stv)))]
    for copy in loads:
        copy.start()

    deltas = [
        (a, b, d, e, f)
        for a in range(YH) for b in range(Z) for d in range(X) for e in range(2) for f in range(p.TP)
        if a + b + d + e + f
    ]

    def away(a, b, d, e, f):
        return {
            "yh": mod(yh + a, YH), "z": mod(z + b, Z), "x": mod(x + d, X),
            "core": mod(c + e, 2), "tp": mod(tp + f, p.TP),
        }

    barrier = pltpu.get_barrier_semaphore()
    for delta in deltas:
        pl.semaphore_signal(barrier, inc=1, device_id=away(*delta), device_id_type=MESH)

    lane = lax.broadcasted_iota(jnp.int32, (1, 128), 1)
    low = lane < HEAD_DIM
    for copy in loads:
        copy.wait()
    for b in range(Z):
        pack[b, :, 0 : p.qc] = stq[:, b * p.qc : (b + 1) * p.qc]
        both = slice(b // 2 * 128, b // 2 * 128 + 128)
        key, val = stk[:, both].astype(F32), stv[:, both].astype(F32)
        if b % 2:
            pair = jnp.where(low, pltpu.roll(key, 64, 1), val)
        else:
            pair = jnp.where(low, key, pltpu.roll(val, 64, 1))
        pack[b, :, p.qc : p.qc + 128] = pair.astype(BF16)
    pl.semaphore_wait(barrier, len(deltas))

    gain_peers = [d for d in deltas if d[4] == 0]
    gbuf[ctx_me] = gin[...]
    for n, src in enumerate((tok, cot)):
        send(src.at[pl.ds(row_of(1 - c, H), H)], swap.at[n], p.swap_s + n, p.swap_r + n, sib)
    for n, delta in enumerate(gain_peers):
        send(gin, gbuf.at[ctx_me], p.gain_s + n, p.gain_r, away(*delta))

    def seg(a, b, d):
        return pl.ds(pl.multiple_of(ctx_of(a, b, d, 0) * R, 2 * R), 2 * R)

    def block(a, b, d, e):
        return pl.ds(pl.multiple_of(ctx_of(a, b, d, e) * R, R), R)

    def piece(i, zz, cc):
        if i == 0:
            return pack.at[zz]
        n = p.cols[i]
        return win[i].at[:, pl.ds(row_of(zz * 2 + cc if i in WIDE else zz, n), n)]

    def s1r(i, d, e):
        return p.s1_r + (i * Z + d) * 2 + e

    def w_stage1(i, steps=None):
        dst = w[i].at[block(yh, z, x, c)]
        for d in range(Z) if steps is None else steps:
            si = p.s1_s + (i * Z + d) * 2
            if i in WIDE:
                for e in range(2):
                    src = piece(i, zplus(d), mod(c + e, 2))
                    if d + e:
                        send(src, dst, si + e, s1r(i, d, c), {"z": zplus(d), "core": mod(c + e, 2)})
                    else:
                        lc(src, dst, p.s1_l + i).start()
                continue
            src = piece(i, zplus(d), c)
            if d == 0:
                pl.when(holder)(lambda: lc(src, dst, p.s1_l + i).start())
            send(src, dst, si, s1r(i, d, c), {"z": zplus(d), "core": tp}, other if d == 0 else None)

    plane = [(a, d, f) for a in range(YH) for d in range(X) for f in range(2) if a + d + f]
    line = [(a, d) for a in range(YH) for d in range(X) if a + d]

    def w_forward(i, steps=None):
        def arrived(d):
            zs = zminus(d)
            if d == 0:
                lc(piece(i, z, c), w[i].at[block(yh, z, x, c)], p.s1_l + i).wait()
                wait_recv(w[i].at[block(yh, z, x, 1 - c)], s1r(i, 0, 1 - c))
            else:
                for e in range(2):
                    wait_recv(w[i].at[block(yh, zs, x, e)], s1r(i, d, e))

        for d in range(Z) if steps is None else steps:
            when(None if i in WIDE else holder, lambda: arrived(d))
            part = w[i].at[seg(yh, zminus(d), x)]
            for n, peer in enumerate(line if i in WIDE else plane):
                send(
                    part, part, p.s2_s + (i * Z + d) * S + n,
                    p.s2_r + (i * YX + peer[0] * X + peer[1]) * Z + d,
                    away(peer[0], 0, peer[1], 0, 0 if i in WIDE else peer[2]),
                    None if i in WIDE else holder,
                )

    def w_wait(i):
        for a in range(YH):
            for dx in range(X):
                def wait_all():
                    for d in range(Z):
                        part = w[i].at[seg(mod(yh + YH - a, YH), zminus(d), mod(x + X - dx, X))]
                        wait_recv(part, p.s2_r + (i * YX + a * X + dx) * Z + d)
                if a + dx:
                    wait_all()
                elif i not in WIDE:
                    pl.when(other)(wait_all)

    def rows_at(g, e, b):
        return pl.ds(pl.multiple_of(((g * 2 + e) * Z + b) * H, H), H)

    up_z, down_z = jnp.minimum(z + 1, Z - 1), jnp.maximum(z - 1, 0)

    def ag_step(k, buf, dist, wide):
        g = tp if wide else 0
        rbase, sbase = p.ag_r + k * 4 * Z, p.ag_s + k * 5 * Z
        if dist == 0:
            mine = buf.at[rows_at(g, c, z)]
            send(mine, mine, sbase + z, rbase + z, {"z": up_z}, z < Z - 1)
            send(mine, mine, sbase + 4 * Z + z, rbase + z, {"z": down_z}, z > 0)
            send(mine, mine, sbase + Z + z, rbase + Z + z, sib)
            if wide:
                send(mine, mine, sbase + 2 * Z + z, rbase + 2 * Z + z, {"tp": 1 - tp})
            return
        for sign in (-1, 1):
            there = z + sign * dist
            has = (there >= 0) & (there < Z)
            b = jnp.clip(there, 0, Z - 1)
            part = buf.at[rows_at(g, c, b)]
            pl.when(has)(lambda: wait_recv(part, rbase + b))
            if dist < Z - 1:
                if sign < 0:
                    send(part, part, sbase + b, rbase + b, {"z": up_z}, has & (z < Z - 1))
                else:
                    send(part, part, sbase + b, rbase + b, {"z": down_z}, has & (z > 0))
            send(part, part, sbase + Z + b, rbase + Z + b, sib, has)
            if wide:
                send(part, part, sbase + 2 * Z + b, rbase + 2 * Z + b, {"tp": 1 - tp}, has)

    def ag_tail(k, buf, wide):
        g = tp if wide else 0
        rbase, sbase = p.ag_r + k * 4 * Z, p.ag_s + k * 5 * Z
        for b in range(Z):
            wait_recv(buf.at[rows_at(g, 1 - c, b)], rbase + Z + b)
        if not wide:
            return
        for b in range(Z):
            part = buf.at[rows_at(1 - tp, c, b)]
            wait_recv(part, rbase + 2 * Z + b)
            send(part, part, sbase + 3 * Z + b, rbase + 3 * Z + b, sib)
        for b in range(Z):
            wait_recv(buf.at[rows_at(1 - tp, 1 - c, b)], rbase + 3 * Z + b)

    def gather(k, buf, wide):
        for dist in range(1, Z):
            ag_step(k, buf, dist, wide)
        ag_tail(k, buf, wide)

    CW = p.model // CHUNKS
    used = {}

    def reuse(name, k):
        before = used.get(name)
        used[name] = k
        return before

    def brecv(k):
        return brecvs.at[0 if k == 1 else 1]

    def groups(k):
        return 2 if k in (1, 2) else 1

    def bsent(k, j):
        wait_send(bsend.at[j, pl.ds(0, groups(k))], p.rb_s + k * CHUNKS + j)

    def ysent(k, j):
        wait_send(ysend.at[j], p.ry_s + k * CHUNKS + j)

    def product(terms, j, g, e):
        rows = pl.ds(pl.multiple_of((g * 2 + e) * HALF, HALF), HALF)
        cols = pl.ds(pl.multiple_of(j * CW, CW), CW)
        total = None
        for a, b in terms:
            part = dot(a[rows, :], b[cols, :], NT)
            total = part if total is None else total + part
        return total

    def own_at(j):
        return pl.ds(pl.multiple_of(j * HALF, HALF), HALF)

    def owns(k):
        return up if k == 2 else gate

    def rs_parts(k, terms):
        wide = groups(k) == 2
        mine = tp if wide else 0
        before_b = reuse("b", k)
        before_y = reuse("y", k) if wide else None

        def first(j, carry):
            values = [product(terms, j, g, 1 - c).astype(BF16) for g in range(groups(k))]
            if before_b is not None and before_b != 2:
                bsent(before_b, j)
            for g, value in enumerate(values):
                bsend[j, g] = value
            rc(
                bsend.at[j, pl.ds(0, groups(k))], brecv(k).at[j, pl.ds(0, groups(k))],
                p.rb_s + k * CHUNKS + j, p.rb_r + k * CHUNKS + j, sib,
            ).start()
            return carry

        lax.fori_loop(0, CHUNKS, first, 0)

        def second(j, carry):
            value = product(terms, j, 1 - tp, c) if wide else None
            wait_recv(brecv(k).at[j, pl.ds(0, groups(k))], p.rb_r + k * CHUNKS + j)
            owns(k)[own_at(j), :] = product(terms, j, mine, c) + brecv(k)[j, mine].astype(F32)
            if not wide:
                return carry
            if before_y is not None:
                ysent(before_y, j)
            ysend[j] = (value + brecv(k)[j, 1 - tp].astype(F32)).astype(BF16)
            rc(
                ysend.at[j], yrecv.at[k - 1, j], p.ry_s + k * CHUNKS + j, p.ry_r + k * CHUNKS + j, {"tp": 1 - tp}
            ).start()
            return carry

        lax.fori_loop(0, CHUNKS, second, 0)

    def rz_r(k, j, t):
        return p.rz_r + (k * CHUNKS + j) * (Z + 1) + t

    def zsent(k, j, t):
        wait_send(zsend.at[j, t], p.rz_s + (k * CHUNKS + j) * Z + t)

    def zslot(k):
        return zrecv.at[k % 3]

    def add_y(k, j):
        if groups(k) == 2:
            wait_recv(yrecv.at[k - 1, j], p.ry_r + k * CHUNKS + j)
            owns(k)[own_at(j), :] += yrecv[k - 1, j].astype(F32)

    def rs_ring(k, between):
        before = reuse("z", k)

        def move(j, t, near):
            upward = z < t
            has = jnp.where(upward, z > 0, z < Z - 1)
            mine = owns(k).at[pl.ds(j * HALF + t * H, H)]

            @pl.when((z != t) & (jnp.where(upward, z < Z // 2, z >= Z // 2) == near))
            def _():
                if before is not None:
                    zsent(before, j, t)

                @pl.when(has)
                def _():
                    wait_recv(zslot(k).at[j, t], rz_r(k, j, t))
                    zsend[j, t] = (mine[...] + zslot(k)[j, t].astype(F32)).astype(BF16)

                @pl.when(jnp.logical_not(has))
                def _():
                    zsend[j, t] = mine[...].astype(BF16)

                to = jnp.where(upward, up_z, down_z)
                slot = jnp.where((to == t) & jnp.logical_not(upward), Z, t)
                rc(
                    zsend.at[j, t], zslot(k).at[j, slot],
                    p.rz_s + (k * CHUNKS + j) * Z + t, rz_r(k, j, slot), {"z": to},
                ).start()

        order = (Z - 1, 0, *range(Z - 2, 0, -1))
        for j in range(CHUNKS + 1):
            if j < CHUNKS:
                add_y(k, j)
                for t in order:
                    move(j, t, True)
            if j:
                for t in order:
                    move(j - 1, t, False)
            if j < CHUNKS:
                between(j)

    def rs_finish(k):
        for j in range(CHUNKS):
            cols = slice(j * CW, (j + 1) * CW)
            acc[:, cols] = owns(k)[pl.ds(pl.multiple_of(j * HALF + z * H, H), H), :]

            @pl.when(z > 0)
            def _():
                wait_recv(zslot(k).at[j, z], rz_r(k, j, z))
                acc[:, cols] += zslot(k)[j, z].astype(F32)

            @pl.when(z < Z - 1)
            def _():
                wait_recv(zslot(k).at[j, Z], rz_r(k, j, Z))
                acc[:, cols] += zslot(k)[j, Z].astype(F32)
        return acc[...]

    def rs_direct(k, chunks):
        for j in chunks:
            bsent(k, j)
            add_y(k, j)
            bsend[j, 1] = owns(k)[own_at(j), :].astype(BF16)
            for d in range(1, Z):
                send(
                    bsend.at[j, 1, pl.ds(row_of(zplus(d), H), H)], zslot(k).at[j, d],
                    p.rz_s + (k * CHUNKS + j) * Z + d, rz_r(k, j, d), {"z": zplus(d)},
                )

    def rs_direct_finish(k):
        parts = []
        for j in range(CHUNKS):
            value = owns(k)[pl.ds(pl.multiple_of(j * HALF + z * H, H), H), :]
            for d in range(1, Z):
                wait_recv(zslot(k).at[j, d], rz_r(k, j, d))
                value = value + zslot(k)[j, d].astype(F32)
            parts.append(value)
        return jnp.concatenate(parts, axis=1)

    per = 256 // (2 * R)

    def dw_place(i, g):
        xd, zd, yd = mod(g, X), mod(lax.div(g, jnp.int32(X)), Z), lax.div(g, jnp.int32(X * Z))
        mine = (xd == x) & (yd == yh)
        return xd, zd, yd, mine if i in WIDE else mine & holder

    def dw_send(many, rows_ref, grads):
        def one(t, carry):
            cols = pl.ds(pl.multiple_of(t * 256, 256), 256)
            left = rows_ref[:, cols]
            for i, grad in zip(many, grads):
                w[i][cols, :] = dot(left, grad[...], TN).astype(BF16)
                for n in range(per):
                    g = t * per + n
                    xd, zd, yd, mine = dw_place(i, g)
                    from_me = yx_me if i in WIDE else s_me

                    @pl.when(jnp.logical_not(mine))
                    def _():
                        rc(
                            w[i].at[pl.ds(pl.multiple_of(g * 2 * R, 2 * R), 2 * R)], rb[i].at[from_me, zd],
                            p.dw_s + i * p.nseg + g, p.dw_r + (i * S + from_me) * Z + zd,
                            {"yh": yd, "x": xd, "tp": tp if i in WIDE else c},
                        ).start()
            return carry

        lax.fori_loop(0, p.model // 256, one, 0)

    def dw_sent(i):
        for g in range(p.nseg):
            mine = dw_place(i, jnp.int32(g))[3]

            @pl.when(jnp.logical_not(mine))
            def _():
                wait_send(w[i].at[pl.ds(g * 2 * R, 2 * R)], p.dw_s + i * p.nseg + g)

    def place(i, zz, cc):
        if i == 0:
            return og[0].at[zz]
        n = p.cols[i]
        return og[i].at[:, pl.ds(row_of(zz * 2 + cc if i in WIDE else zz, n), n)]

    def ogr(i, zz, cc):
        return p.og_r + (i * Z + zz) * 2 + (cc if i in WIDE else 0)

    def dw_reduce(i, zds=None):
        n = p.cols[i]
        size, me = (YX, yx_me) if i in WIDE else (S, s_me)
        items = [(zd, at, min(TMP, n - at)) for zd in (range(Z) if zds is None else zds) for at in range(0, n, TMP)]

        def tiles(q):
            zd, at, width = items[q]
            return [
                lc(
                    rb[i].at[mod(me + d, size), zd, :, pl.ds(at, width)],
                    tmp.at[q % 2, d - 1, :, pl.ds(0, width)], p.tmp_l + q % 2 * S + d,
                )
                for d in range(1, size)
            ]

        def begin(q):
            zd, at, _ = items[q]
            if at == 0:
                for d in range(1, size):
                    s = mod(me + d, size)
                    wait_recv(rb[i].at[s, zd], p.dw_r + (i * S + s) * Z + zd)
            for copy in tiles(q):
                copy.start()

        def run():
            begin(0)
            for q, (zd, at, width) in enumerate(items):
                if q + 1 < len(items):
                    begin(q + 1)
                for copy in tiles(q):
                    copy.wait()
                mine = seg(yh, zd, x)
                total = w[i][mine, at : at + width].astype(F32)
                for d in range(1, size):
                    total = total + tmp[q % 2, d - 1, :, 0:width].astype(F32)
                w[i][mine, at : at + width] = total.astype(BF16)
                if at + width < n:
                    continue
                for e in range(2):
                    src = w[i].at[block(yh, zd, x, e)]
                    here = (z == zd) & (c == e)

                    @pl.when(here)
                    def _():
                        lc(src, place(i, z, c), p.og_l + i).start()

                    @pl.when(jnp.logical_not(here))
                    def _():
                        rc(
                            src, place(i, z, c), p.og_s + (i * Z + zd) * 2 + e, ogr(i, z, c),
                            {"z": jnp.int32(zd), "core": jnp.int32(e)},
                        ).start()

        when(None if i in WIDE else holder, run)

    def dw_done(i):
        cores = range(2) if i in WIDE else (0,)
        for b in range(Z):
            for e in cores:
                here = (z == b) & ((c == e) if i in WIDE else holder)

                @pl.when(here)
                def _():
                    lc(w[i].at[block(yh, z, x, c)], place(i, z, c), p.og_l + i).wait()

                @pl.when(jnp.logical_not(here))
                def _():
                    wait_recv(place(i, jnp.int32(b), jnp.int32(e)), ogr(i, b, e))

        def sent():
            for zd in range(Z):
                for e in range(2):
                    @pl.when(jnp.logical_not((z == zd) & (c == e)))
                    def _():
                        wait_send(w[i].at[block(yh, zd, x, e)], p.og_s + (i * Z + zd) * 2 + e)

        when(None if i in WIDE else holder, sent)

    def deliver(k, out):
        dst = out.at[pl.ds(row_of(c, H), H)]
        for t in range(p.TP):
            here = holder & (tp == t)
            pl.when(here)(lambda: lc(swap.at[k], dst, p.out_l + k).start())
            send(
                swap.at[k], dst, p.out_s + k * 2 + t, p.out_r + k * 2 + c,
                {"core": tp, "tp": jnp.int32(t)}, jnp.logical_not(here),
            )

    def delivered(k, out):
        for e in range(2):
            here = holder & (c == e)

            @pl.when(here)
            def _():
                lc(swap.at[k], out.at[pl.ds(row_of(c, H), H)], p.out_l + k).wait()

            @pl.when(jnp.logical_not(here))
            def _():
                wait_recv(out.at[pl.ds(e * H, H)], p.out_r + k * 2 + e)

    def fill(point):
        for kind, *args in FILL.get(point, ()):
            if kind == "stage":
                w_stage1(args[0], args[1])
            elif kind == "forward":
                w_forward(args[0], args[1])
            elif kind == "cotangent":
                ag_step(1, gg, args[0], True)
            elif kind == "sum":
                rs_direct(2, args[0])
            else:
                dw_reduce(args[0], args[1])

    w_stage1(0)
    for n in range(2):
        wait_recv(swap.at[n], p.swap_r + n)
    mine = pl.ds(row_of(c, H), H)
    toks[...] = jnp.where(holder, tok[mine, :], swap[0])
    gg[rows_at(tp, c, z), :] = jnp.where(holder, cot[mine, :], swap[1])
    token_rows = toks[...].astype(F32)
    fill("inputs")
    factor_attn = lax.rsqrt(jnp.mean(token_rows * token_rows, axis=1, keepdims=True) + EPS)
    wait_recv(gbuf.at[pl.ds(0, p.n_ctx - 1)], p.gain_r)
    q = p.n_ctx * 128 // p.model
    gain_parts = []
    for b in range(p.model // 128):
        total = gbuf[b * q]
        for n in range(1, q):
            total = total + gbuf[b * q + n]
        gain_parts.append(total)
    gains = jnp.concatenate(gain_parts, axis=1)
    gain_attn, gain_mlp = gains[0:1, :], gains[1:2, :]
    n1[rows_at(0, c, z), :] = (token_rows * factor_attn * gain_attn).astype(BF16)
    ag_step(0, n1, 0, False)
    fill("n1_0")
    w_forward(0)
    ag_step(0, n1, 1, False)
    fill("n1_1")
    ag_step(0, n1, 2, False)
    fill("n1_2")
    ag_step(0, n1, 3, False)
    ag_tail(0, n1, False)
    fill("n1_3")
    w_wait(0)

    first_half = mod(lane, HEAD_DIM) < HEAD_DIM // 2

    def rotate(t, cosine, sine):
        turned = jnp.where(first_half, pltpu.roll(t, 96, 1), pltpu.roll(t, 32, 1))
        return t * cosine + turned * sine

    lin = dot(n1[...], w0[...], NN)
    cosine, sine = cosr[...], sinr[...]
    scale = HEAD_DIM ** (-0.5)
    pairs = p.qc // 128
    kv_lin = lin[:, p.qc : p.qc + 128]
    own_rows = pl.ds(pl.multiple_of(s_me * p.rows, p.rows), p.rows)
    kvall[own_rows, :] = jnp.where(low, rotate(kv_lin, cosine, sine), kv_lin).astype(BF16)
    for n, (a, dx, f) in enumerate(plane):
        send(kvall.at[own_rows], kvall.at[own_rows], p.kv_s + n, p.kv_r + n, away(a, 0, dx, 0, f))
    for n in range(pairs):
        turned_q = rotate(lin[:, n * 128 : (n + 1) * 128], cosine, sine).astype(BF16).astype(F32) * scale
        qpad[2 * n] = jnp.where(low, turned_q, 0.0).astype(BF16)
        qpad[2 * n + 1] = jnp.where(low, pltpu.roll(turned_q, 64, 1), 0.0).astype(BF16)

    def from_plane(a, dx, f):
        s = (mod(yh + YH - a, YH) * X + mod(x + X - dx, X)) * 2 + mod(tp + 2 - f, 2)
        return pl.ds(pl.multiple_of(s * p.rows, p.rows), p.rows)

    fill("kv")
    for n, delta in enumerate(plane):
        wait_recv(kvall.at[from_plane(*delta)], p.kv_r + n)
    fill("attend_0")
    T = p.tile
    KC = p.rows
    down = lax.broadcasted_iota(jnp.int32, (BLOCK, 1), 0)

    def masked(s, rows, scores):
        at = posq[:, rows]
        parts = []
        for b in range(2 * Z):
            allowed = down <= at - ids[s, b] * BLOCK
            parts.append(jnp.where(allowed, scores[b * BLOCK : (b + 1) * BLOCK, :], NEG))
        return jnp.concatenate(parts, axis=0)

    def keys(s):
        return pl.ds(s * KC, KC)

    for n in range(pairs):
        def attend(t, carry):
            rows = pl.ds(pl.multiple_of(t * T, T), T)
            outs = []
            for e in range(2):
                h = 2 * n + e
                query = qpad[h, rows, :]
                top = jnp.full((8, T), NEG, F32)
                for s in range(S):
                    scores = masked(s, rows, dot(kvall[keys(s), :], query, NT))
                    dkv[keys(s), :] = scores
                    top = jnp.maximum(top, jnp.max(scores.reshape(KC // 8, 8, T), axis=0))
                top = jnp.max(top, axis=0, keepdims=True)
                total = jnp.zeros((8, T), F32)
                for s in range(S):
                    grown = jnp.exp(dkv[keys(s), :] - top)
                    dkv[keys(s), :] = grown
                    total = total + jnp.sum(grown.reshape(KC // 8, 8, T), axis=0)
                total = jnp.sum(total, axis=0, keepdims=True)
                lse[h : h + 1, rows] = top + jnp.log(total)
                share = 1.0 / total
                out = jnp.zeros((128, T), F32)
                for s in range(S):
                    out = out + dot(kvall[keys(s), :], (dkv[keys(s), :] * share).astype(BF16), TN)
                outs.append(out[HEAD_DIM:, :])
            out = jnp.concatenate(outs, axis=0)
            ot[n, :, rows] = out
            mixed[rows, n * 128 : (n + 1) * 128] = jnp.transpose(out).astype(BF16)
            return carry

        lax.fori_loop(0, p.rows // T, attend, 0)
        fill(f"attend_{n + 1}")
    w_wait(1)
    rs_parts(0, [(mixed, w1)])
    rs_ring(0, lambda j: fill(f"residual_{j}"))
    residual = toks[...].astype(F32) + rs_finish(0)
    resid[...] = residual
    factor_mlp = lax.rsqrt(jnp.mean(residual * residual, axis=1, keepdims=True) + EPS)
    n2[rows_at(tp, c, z), :] = (residual * factor_mlp * gain_mlp).astype(BF16)
    ag_step(2, n2, 0, True)
    fill("n2_0")
    ag_step(2, n2, 1, True)
    fill("n2_1")
    ag_step(2, n2, 2, True)
    fill("n2_2")
    ag_step(2, n2, 3, True)
    ag_tail(2, n2, True)
    fill("n2_3")

    w_wait(2)
    w_wait(3)

    def feed(t, carry):
        cols = pl.ds(pl.multiple_of(t * 256, 256), 256)
        gate[:, cols] = dot(n2[...], w2[:, cols], NN)
        up[:, cols] = dot(n2[...], w3[:, cols], NN)
        return carry

    lax.fori_loop(0, p.fc // 256, feed, 0)
    fill("feed")
    ag_tail(1, gg, True)
    w_wait(4)

    def feed_back(t, carry):
        cols = pl.ds(pl.multiple_of(t * 256, 256), 256)
        back = dot(gg[...], w4[:, cols], NN)
        gate_pre, up_pre = gate[:, cols], up[:, cols]
        sig = jax.nn.sigmoid(gate_pre)
        silu = gate_pre * sig
        hid[:, cols] = (silu * up_pre).astype(BF16)
        dgate[:, cols] = (back * up_pre * sig * (1.0 + gate_pre * (1.0 - sig))).astype(BF16)
        dup[:, cols] = (back * silu).astype(BF16)
        return carry

    lax.fori_loop(0, p.fc // 256, feed_back, 0)
    drain = pending[:]
    pending.clear()
    for wait in drain:
        wait()
    norm_terms, out_terms = [(dgate, w2), (dup, w3)], [(hid, w4)]
    rs_parts(1, norm_terms)
    rs_parts(2, out_terms)
    for i, left, right in ((4, gg, hid), (2, n2, dgate), (3, n2, dup)):
        dw_send([i], left, [right])
    rs_ring(1, lambda j: fill(f"norm_{j}"))
    grad_norm_mlp = rs_finish(1)
    weighted = grad_norm_mlp * gain_mlp
    u = resid[...] * factor_mlp
    grad_residual = gg[rows_at(tp, c, z), :].astype(F32) + factor_mlp * (
        weighted - u * jnp.mean(weighted * u, axis=1, keepdims=True)
    )
    gain_mlp_part = jnp.sum(grad_norm_mlp * u, axis=0, keepdims=True)
    ga[rows_at(0, c, z), :] = grad_residual.astype(BF16)
    resid2[...] = grad_residual
    ag_step(3, ga, 0, False)
    fill("ga_0")
    ag_step(3, ga, 1, False)
    fill("ga_1")
    ag_step(3, ga, 2, False)
    fill("ga_2")
    ag_step(3, ga, 3, False)
    ag_tail(3, ga, False)
    fill("ga_3")

    for n in range(pairs):
        gm = dot(ga[...], w1[:, n * 128 : (n + 1) * 128], NN).astype(BF16).astype(F32)
        ot[n] = ot[n] * jnp.transpose(gm)
        gmpad[2 * n] = jnp.where(low, 0.0, pltpu.roll(gm, 64, 1)).astype(BF16)
        gmpad[2 * n + 1] = jnp.where(low, 0.0, gm).astype(BF16)
    dw_send([1], ga, [mixed])
    fill("back_0")
    dkv[:, 0:128] = jnp.zeros((p.seq, 128), F32)
    for n in range(pairs):
        def attend_back(t, carry):
            rows = pl.ds(pl.multiple_of(t * T, T), T)
            agree = ot[n, :, rows]
            outs = []
            for e in range(2):
                h = 2 * n + e
                query, back = qpad[h, rows, :], gmpad[h, rows, :]
                level = lse[h : h + 1, rows]
                delta = jnp.sum(agree[e * HEAD_DIM : (e + 1) * HEAD_DIM, :], axis=0, keepdims=True)
                out = jnp.zeros((128, T), F32)
                for s in range(S):
                    here = kvall[keys(s), :]
                    probs = jnp.exp(masked(s, rows, dot(here, query, NT)) - level)
                    ds = (probs * (dot(here, back, NT) - delta)).astype(BF16)
                    out = out + dot(here, ds, TN)
                    dkv[keys(s), 0:128] += dot(ds, query, NN) + dot(probs.astype(BF16), back, NN)
                outs.append(out[:HEAD_DIM, :])
            dq[rows, n * 128 : (n + 1) * 128] = jnp.transpose(jnp.concatenate(outs, axis=0)) * scale
            return carry

        lax.fori_loop(0, p.rows // T, attend_back, 0)
        fill(f"back_{n + 1}")
    dkv_own = dkv[own_rows, 0:128]
    for s in range(S):
        kvall[keys(s), :] = dkv[keys(s), 0:128].astype(BF16)
    for n, (a, dx, f) in enumerate(plane):
        s = (mod(yh + a, YH) * X + mod(x + dx, X)) * 2 + mod(tp + f, 2)
        send(
            kvall.at[pl.ds(pl.multiple_of(s * p.rows, p.rows), p.rows)], dkvr.at[n],
            p.dkv_s + n, p.dkv_r + n, away(a, 0, dx, 0, f),
        )
    fill("terms")
    for n in range(pairs):
        cols = slice(n * 128, (n + 1) * 128)
        gqkv[:, cols] = rotate(dq[:, cols], cosr[...], -sinr[...]).astype(BF16)
    for n in range(len(plane)):
        wait_recv(dkvr.at[n], p.dkv_r + n)
        dkv_own = dkv_own + dkvr[n].astype(F32)
    gqkv[:, p.qc : p.qc + 128] = jnp.where(low, rotate(dkv_own, cosr[...], -sinr[...]), dkv_own).astype(BF16)
    rs_parts(3, [(gqkv, w0)])
    dw_send([0], n1, [gqkv])
    rs_ring(3, lambda j: fill(f"input_{j}"))
    grad_norm_attn = rs_finish(3)
    weighted = grad_norm_attn * gain_attn
    scaled_attn = toks[...].astype(F32) * factor_attn
    swap[1] = (
        resid2[...] + factor_attn * (weighted - scaled_attn * jnp.mean(weighted * scaled_attn, axis=1, keepdims=True))
    ).astype(BF16)
    deliver(1, in_grad)

    gain_attn_part = jnp.sum(grad_norm_attn * scaled_attn, axis=0, keepdims=True)
    both_gains = jnp.concatenate([gain_attn_part, gain_mlp_part, jnp.zeros((6, p.model), F32)], axis=0)
    for b in range(p.model // 128):
        ggs[b] = both_gains[:, b * 128 : (b + 1) * 128]
    dev_me = ctx_me * p.TP + tp
    ggr[dev_me] = ggs[lax.div(ctx_me * R, jnp.int32(128))]
    for n, delta in enumerate(deltas):
        to = away(*delta)
        there = ctx_of(to["yh"], to["z"], to["x"], to["core"])
        send(ggs.at[lax.div(there * R, jnp.int32(128))], ggr.at[dev_me], p.gg_s + n, p.gg_r, to)

    fill("end_0")
    swap[0] = (resid[...] + rs_direct_finish(2)).astype(BF16)
    deliver(0, block_out)
    fill("end_1")
    wait_recv(ggr.at[pl.ds(0, p.n_dev - 1)], p.gg_r)
    total = ggr[0]
    for n in range(1, p.n_dev):
        total = total + ggr[n]
    gain_grad[...] = total

    for i in (4, 2, 3, 1, 0):
        dw_sent(i)
        dw_done(i)
    delivered(0, block_out)
    delivered(1, in_grad)
    for wait in pending:
        wait()

    def last(j, carry):
        bsent(3, j)
        ysent(2, j)
        for t in range(Z):
            pl.when(z != t)(lambda: zsent(used["z"], j, t))
        return carry

    lax.fori_loop(0, CHUNKS, last, 0)


def local(sizes, tokens, block_ids, gain_attn, w_query, key_weight, value_weight, w_out, gain_mlp,
          w_gate, w_up, w_down, cotangent):
    row_count, model = tokens.shape
    p = Plan(sizes, model, w_query.shape[1], key_weight.shape[1], w_gate.shape[1], row_count)
    YH, Z, X, S, R = p.YH, p.Z, p.X, p.S, p.R
    yh, z, x, c, tp = (lax.axis_index(a) for a in AXES)
    ctx_me = ((yh * Z + z) * X + x) * 2 + c
    s_me = (yh * X + x) * 2 + tp
    ids = block_ids.reshape(YH, Z, X, 2, 2).transpose(0, 2, 3, 4, 1).reshape(S, 2 * Z)
    positions = (ids[:, :, None] * BLOCK + jnp.arange(BLOCK, dtype=jnp.int32)).reshape(S, p.rows)
    own = lax.dynamic_slice_in_dim(positions, s_me, 1, 0)
    half = HEAD_DIM // 2
    frequencies = THETA ** (-(jnp.arange(half, dtype=F32) * 2.0 / HEAD_DIM))
    angles = own.reshape(p.rows, 1).astype(F32) * jnp.tile(frequencies, 4)[None, :]
    signs = jnp.where(jnp.arange(128) % HEAD_DIM < half, -1.0, 1.0).astype(F32)
    cosine, sine = jnp.cos(angles), jnp.sin(angles) * signs
    gains = jnp.stack([gain_attn, gain_mlp]).astype(F32)
    gin = lax.dynamic_update_slice(jnp.zeros((8, 128), F32), gains, (0, lax.rem(ctx_me * R, 128)))
    V = pl.BlockSpec(memory_space=pltpu.VMEM)
    A = pl.BlockSpec(memory_space=pl.ANY)
    H = p.half
    sd = jax.ShapeDtypeStruct
    out_shape = [sd((row_count, model), BF16), sd((row_count, model), BF16), sd((8, 128), F32)]
    out_shape += [sd((Z, R, p.cols[0]), BF16), sd(w_out.shape, BF16)] + [sd(w_gate.shape, BF16)] * 3
    out_shape += [sd((p.YX if i in WIDE else S, Z, 2 * R, n), BF16) for i, n in enumerate(p.cols)]
    CW = model // CHUNKS
    assert CW == p.fc and CHUNKS * Z * H == p.wide_rows
    scratch = [
        pltpu.VMEM((p.n_ctx, 8, 128), F32),
        pltpu.VMEM((2, H, model), BF16),
        *[pltpu.VMEM(a.shape, BF16) for a in (w_query, key_weight, value_weight)],
        pltpu.VMEM((Z, R, p.cols[0]), BF16),
        *[pltpu.VMEM((n, model), BF16) for n in (p.rows, p.wide_rows, p.wide_rows, p.rows)],
        *[pltpu.VMEM((model, n), BF16) for n in p.cols],
        pltpu.VMEM((p.qc // 64, p.rows, 128), BF16),
        pltpu.VMEM((p.qc // 64, p.rows, 128), BF16),
        pltpu.VMEM((p.seq, 128), BF16),
        pltpu.VMEM((p.seq, p.tile), F32),
        pltpu.VMEM((8, p.rows), F32),
        pltpu.VMEM((p.qc // 128, 128, p.rows), F32),
        pltpu.VMEM((p.rows, p.qc), BF16),
        *[pltpu.VMEM((p.wide_rows, p.fc), BF16) for _ in range(3)],
        *[pltpu.VMEM((p.wide_rows, p.fc), F32) for _ in range(2)],
        pltpu.VMEM((p.rows, p.qc), F32),
        pltpu.VMEM((S - 1, p.rows, 128), BF16),
        pltpu.VMEM((p.rows, p.cols[0]), BF16),
        pltpu.VMEM((CHUNKS, 2, Z * H, CW), BF16),
        pltpu.VMEM((2, CHUNKS, 2, Z * H, CW), BF16),
        pltpu.VMEM((CHUNKS, Z * H, CW), BF16),
        pltpu.VMEM((2, CHUNKS, Z * H, CW), BF16),
        pltpu.VMEM((CHUNKS, Z, H, CW), BF16),
        pltpu.VMEM((3, CHUNKS, Z + 1, H, CW), BF16),
        pltpu.VMEM((H, model), F32),
        pltpu.VMEM((H, model), BF16),
        pltpu.VMEM((H, model), F32),
        pltpu.VMEM((H, model), F32),
        pltpu.VMEM((model // 128, 8, 128), F32),
        pltpu.VMEM((p.n_dev, 8, 128), F32),
        pltpu.VMEM((2, S - 1, 2 * R, TMP), BF16),
        pltpu.SemaphoreType.DMA((p.n_send,)),
        pltpu.SemaphoreType.DMA((p.n_recv,)),
        pltpu.SemaphoreType.DMA((p.n_local,)),
    ]
    outs = pl.pallas_call(
        lambda *refs: block_kernel(p, *refs),
        out_shape=out_shape,
        in_specs=[V] * 6 + [pl.BlockSpec(memory_space=pltpu.SMEM)] + [A] * 7,
        out_specs=[A, A, V] + [A] * 10,
        scratch_shapes=scratch,
        compiler_params=pltpu.CompilerParams(
            collective_id=0, has_side_effects=True, vmem_limit_bytes=65400 * 1024
        ),
        name="block",
    )(
        tokens, cotangent, gin, cosine, sine, own, ids,
        w_query, key_weight, value_weight, w_out, w_gate, w_up, w_down,
    )
    block_out, in_grad, gain_grad = outs[:3]
    g_out, g_gate, g_up, g_down = (g.astype(F32) for g in outs[4:8])
    g_qkv = outs[3].transpose(1, 0, 2).astype(F32)
    gain_grads = lax.dynamic_slice(gain_grad, (0, lax.rem(ctx_me * R, 128)), (2, R))
    return (
        block_out,
        in_grad,
        gain_grads[0],
        g_qkv[:, :, : p.qc].reshape(R, -1),
        g_qkv[:, :, p.qc : p.qc + p.kc].reshape(R, -1),
        g_qkv[:, :, p.qc + p.kc :].reshape(R, -1),
        g_out,
        gain_grads[1],
        g_gate,
        g_up,
        g_down,
    )


def solution(mesh):
    n_ctx, tp = mesh.devices.shape
    Z = 4
    X = 2 if n_ctx == 16 else 4
    YH = n_ctx // (Z * X * 2)
    sizes = (YH, Z, X, tp)
    split = Mesh(mesh.devices.reshape(YH, Z, X, 2, tp), AXES)
    ctx = AXES[:4]
    rows, weight, vector = P(ctx, None), P(ctx, "tp"), P(ctx)
    return jax.shard_map(
        lambda *args: local(sizes, *args),
        mesh=split,
        in_specs=(rows, P(), vector, weight, weight, weight, weight, vector, weight, weight, weight, rows),
        out_specs=(rows, rows, vector, weight, weight, weight, weight, vector, weight, weight, weight),
        check_vma=False,
    )
```

time: 521 us -> 413 us (0.79)
  Pallas kernels: 482 us -> 392 us
  local copies, waits for them, and re-layouts: 27.2 us -> 7.24 us
    pallas_call x1, Pallas kernels: 482 us -> 392 us  [local(): pl.pallas_call(lambda *refs: block_kernel(p, *refs), out_shape=out_shape,...]
    unnamed x24 -> x17, local copies, waits for them, and re-layouts: 17 us -> 4.12 us
    convert_element_type x1 -> x5, other arithmetic: 0.05 us -> 7.42 us  [the longest x4 6.37 us: local(): g_out, g_gate, g_up, g_down = (g.astype(F32) for g in outs[4:8])]
    reshape x7 -> x0, local copies, waits for them, and re-layouts: 7.12 us -> none  [the longest x1 2.88 us: local(): g_down.reshape(R, -1)]
where the time goes in v2:
time: 413 us; the launch traced here: 411 us
  Pallas kernels  392 us (95%)
  other arithmetic  11.1 us (3%)
  local copies, waits for them, and re-layouts  7.24 us (2%)
    pallas_call x1, Pallas kernels, local(): pl.pallas_call(lambda *refs: block_kernel(p, *refs), out_shape=out_shape,...  392 us

profile of v2, /device:TPU:1, one launch (start us, length us, event | category | flops | bytes accessed | tf_op | source)
XLA Modules:
  0.0 410.8 jit_solution(13224375715323720269)
XLA Ops:
  0.7 0.1 mul.50
  0.8 1.3 fusion.4.refs_2_
  2.0 0.1 add.47
  2.1 0.7 reshape.72
  2.9 0.1 copy.24
  3.0 0.1 broadcast_in_dim_reshape.3.refs_6_
  3.1 0.0 copy-start.5
  3.1 0.1 add.44
  3.1 0.1 add.45
  3.2 0.6 fusion.5
  3.8 1.8 fusion
  5.6 0.0 copy-done.5
  5.6 391.7 %block.1 = (bf16[128,2048]{1,0:T(8,128)(2,1)}, bf16[128,2048]{1,0:T(8,128)(2,1)}, f32[8,128]{1,0:T(8,128)}, bf16[4,128,384]{2,1,0:T(8,128)(2,1)}, bf16[128,1024]...) custom-call(bf16[128,2048]{1,0:T(8,128)(2,1)} %refs_0_.1, ...), custom_call_target="tpu_custom_call" | custom-call | tf_op jit(solution)/shard_map/block/pallas_call | solution.py:986
  397.3 1.3 slice_bitcast_fusion
  398.6 1.8 convert_element_type.34
  400.4 1.0 convert_bitcast_fusion
  401.5 0.0 copy-start.2
  401.5 0.1 fusion.6
  401.7 0.1 copy.27
  401.8 0.8 copy.30
  402.5 0.2 copy.25
  402.7 1.0 copy.28
  403.7 0.0 copy-start.1
  403.7 0.1 copy.26
  403.9 0.8 copy.29
  404.6 0.0 copy-done.2
  404.6 1.5 convert_element_type.35
  406.1 0.0 copy-done.1
  406.1 0.0 copy-start
  406.1 1.5 convert_element_type.36
  407.7 0.0 copy-done
  407.7 0.0 copy-start.4
  407.7 0.0 copy-start.3
  407.7 1.5 convert_element_type.37
  409.2 0.0 copy-done.4
  409.2 0.8 copy.33
  410.0 0.0 copy-done.3
  410.0 0.8 copy.34
  (6 shorter events, 0.1 us)
Async XLA Ops:
  3.1 2.6 copy-start.5
  401.5 3.1 copy-start.2
  403.7 2.4 copy-start.1
  406.1 1.5 copy-start
  407.7 1.5 copy-start.4
  407.7 2.3 copy-start.3

commit v3 on v2

--- a/solution.py
+++ b/solution.py
@@ -21,7 +21,6 @@
 F32 = jnp.float32
 BF16 = jnp.bfloat16
 CHUNKS = 4
-TMP = 128
 WIDE = (2, 3, 4)
 ALL = (0, 1, 2, 3)
 FILL = {
@@ -33,14 +32,15 @@
     "attend_1": [("cotangent", 2), ("forward", 2, ALL), ("stage", 4, ALL)],
     "attend_2": [("cotangent", 3), ("forward", 3, ALL)],
     "n2_2": [("forward", 4, ALL)],
-    "norm_0": [("reduce", 4, (0,))],
-    "norm_1": [("reduce", 4, (1,))],
-    "norm_2": [("reduce", 4, (2,))],
-    "norm_3": [("reduce", 4, (3,))],
-    "ga_0": [("sum", (0, 1))],
-    "ga_1": [("sum", (2, 3))],
-    "ga_3": [("reduce", 2, (0, 1))],
-    "back_0": [("reduce", 2, (2, 3))],
+    "norm_0": [("grad", 4)],
+    "norm_1": [("grad", 2)],
+    "norm_2": [("reduce", 4, (0,)), ("grad", 3)],
+    "norm_3": [("reduce", 4, (1, 2))],
+    "ga_0": [("reduce", 4, (3,)), ("ring", 0)],
+    "ga_1": [("ring", 1)],
+    "ga_2": [("ring", 2)],
+    "ga_3": [("ring", 3), ("reduce", 2, (0, 1))],
+    "back_0": [("ring", 4), ("reduce", 2, (2, 3))],
     "back_1": [("reduce", 3, (0, 1))],
     "back_2": [("reduce", 3, (2, 3))],
     "terms": [("reduce", 1, ALL)],
@@ -84,7 +84,9 @@
         self.wide_rows = 2 * self.rows
         self.seq = self.S * self.rows
         self.nseg = self.n_ctx // 2
-        self.tile = 256 if self.seq <= 2048 else 128
+        self.fast = self.seq <= 2048
+        self.tile = 256 if self.fast else 128
+        self.tmp = 256 if self.fast else 128
         send, recv, local = Sems(), Sems(), Sems()
         W, Z, S, YX = 5, self.Z, self.S, self.YX
         self.gain_s, self.gain_r = send.take(self.n_ctx), recv.take(1)
@@ -364,7 +366,7 @@
 
         def first(j, carry):
             values = [product(terms, j, g, 1 - c).astype(BF16) for g in range(groups(k))]
-            if before_b is not None and before_b != 2:
+            if before_b is not None:
                 bsent(before_b, j)
             for g, value in enumerate(values):
                 bsend[j, g] = value
@@ -406,8 +408,12 @@
             wait_recv(yrecv.at[k - 1, j], p.ry_r + k * CHUNKS + j)
             owns(k)[own_at(j), :] += yrecv[k - 1, j].astype(F32)
 
-    def rs_ring(k, between):
-        before = reuse("z", k)
+    rings = {}
+
+    def ring_step(k, step):
+        if step == 0:
+            rings[k] = reuse("z", k)
+        before = rings[k]
 
         def move(j, t, near):
             upward = z < t
@@ -436,16 +442,19 @@
                 ).start()
 
         order = (Z - 1, 0, *range(Z - 2, 0, -1))
-        for j in range(CHUNKS + 1):
-            if j < CHUNKS:
-                add_y(k, j)
-                for t in order:
-                    move(j, t, True)
-            if j:
-                for t in order:
-                    move(j - 1, t, False)
-            if j < CHUNKS:
-                between(j)
+        if step < CHUNKS:
+            add_y(k, step)
+            for t in order:
+                move(step, t, True)
+        if step:
+            for t in order:
+                move(step - 1, t, False)
+
+    def rs_ring(k, between):
+        for step in range(CHUNKS + 1):
+            ring_step(k, step)
+            if step < CHUNKS:
+                between(step)
 
     def rs_finish(k):
         for j in range(CHUNKS):
@@ -463,27 +472,6 @@
                 acc[:, cols] += zslot(k)[j, Z].astype(F32)
         return acc[...]
 
-    def rs_direct(k, chunks):
-        for j in chunks:
-            bsent(k, j)
-            add_y(k, j)
-            bsend[j, 1] = owns(k)[own_at(j), :].astype(BF16)
-            for d in range(1, Z):
-                send(
-                    bsend.at[j, 1, pl.ds(row_of(zplus(d), H), H)], zslot(k).at[j, d],
-                    p.rz_s + (k * CHUNKS + j) * Z + d, rz_r(k, j, d), {"z": zplus(d)},
-                )
-
-    def rs_direct_finish(k):
-        parts = []
-        for j in range(CHUNKS):
-            value = owns(k)[pl.ds(pl.multiple_of(j * HALF + z * H, H), H), :]
-            for d in range(1, Z):
-                wait_recv(zslot(k).at[j, d], rz_r(k, j, d))
-                value = value + zslot(k)[j, d].astype(F32)
-            parts.append(value)
-        return jnp.concatenate(parts, axis=1)
-
     per = 256 // (2 * R)
 
     def dw_place(i, g):
@@ -491,24 +479,22 @@
         mine = (xd == x) & (yd == yh)
         return xd, zd, yd, mine if i in WIDE else mine & holder
 
-    def dw_send(many, rows_ref, grads):
+    def dw_send(i, rows_ref, grad):
         def one(t, carry):
             cols = pl.ds(pl.multiple_of(t * 256, 256), 256)
-            left = rows_ref[:, cols]
-            for i, grad in zip(many, grads):
-                w[i][cols, :] = dot(left, grad[...], TN).astype(BF16)
-                for n in range(per):
-                    g = t * per + n
-                    xd, zd, yd, mine = dw_place(i, g)
-                    from_me = yx_me if i in WIDE else s_me
-
-                    @pl.when(jnp.logical_not(mine))
-                    def _():
-                        rc(
-                            w[i].at[pl.ds(pl.multiple_of(g * 2 * R, 2 * R), 2 * R)], rb[i].at[from_me, zd],
-                            p.dw_s + i * p.nseg + g, p.dw_r + (i * S + from_me) * Z + zd,
-                            {"yh": yd, "x": xd, "tp": tp if i in WIDE else c},
-                        ).start()
+            w[i][cols, :] = dot(rows_ref[:, cols], grad[...], TN).astype(BF16)
+            for n in range(per):
+                g = t * per + n
+                xd, zd, yd, mine = dw_place(i, g)
+                from_me = yx_me if i in WIDE else s_me
+
+                @pl.when(jnp.logical_not(mine))
+                def _():
+                    rc(
+                        w[i].at[pl.ds(pl.multiple_of(g * 2 * R, 2 * R), 2 * R)], rb[i].at[from_me, zd],
+                        p.dw_s + i * p.nseg + g, p.dw_r + (i * S + from_me) * Z + zd,
+                        {"yh": yd, "x": xd, "tp": tp if i in WIDE else c},
+                    ).start()
             return carry
 
         lax.fori_loop(0, p.model // 256, one, 0)
@@ -533,7 +519,7 @@
     def dw_reduce(i, zds=None):
         n = p.cols[i]
         size, me = (YX, yx_me) if i in WIDE else (S, s_me)
-        items = [(zd, at, min(TMP, n - at)) for zd in (range(Z) if zds is None else zds) for at in range(0, n, TMP)]
+        items = [(zd, at, min(p.tmp, n - at)) for zd in (range(Z) if zds is None else zds) for at in range(0, n, p.tmp)]
 
         def tiles(q):
             zd, at, width = items[q]
@@ -638,8 +624,10 @@
                 w_forward(args[0], args[1])
             elif kind == "cotangent":
                 ag_step(1, gg, args[0], True)
-            elif kind == "sum":
-                rs_direct(2, args[0])
+            elif kind == "ring":
+                ring_step(2, args[0])
+            elif kind == "grad":
+                dw_send(args[0], gg if args[0] == 4 else n2, {4: hid, 2: dgate, 3: dup}[args[0]])
             else:
                 dw_reduce(args[0], args[1])
 
@@ -800,8 +788,6 @@
     norm_terms, out_terms = [(dgate, w2), (dup, w3)], [(hid, w4)]
     rs_parts(1, norm_terms)
     rs_parts(2, out_terms)
-    for i, left, right in ((4, gg, hid), (2, n2, dgate), (3, n2, dup)):
-        dw_send([i], left, [right])
     rs_ring(1, lambda j: fill(f"norm_{j}"))
     grad_norm_mlp = rs_finish(1)
     weighted = grad_norm_mlp * gain_mlp
@@ -827,7 +813,7 @@
         ot[n] = ot[n] * jnp.transpose(gm)
         gmpad[2 * n] = jnp.where(low, 0.0, pltpu.roll(gm, 64, 1)).astype(BF16)
         gmpad[2 * n + 1] = jnp.where(low, 0.0, gm).astype(BF16)
-    dw_send([1], ga, [mixed])
+    dw_send(1, ga, mixed)
     fill("back_0")
     dkv[:, 0:128] = jnp.zeros((p.seq, 128), F32)
     for n in range(pairs):
@@ -871,7 +857,7 @@
         dkv_own = dkv_own + dkvr[n].astype(F32)
     gqkv[:, p.qc : p.qc + 128] = jnp.where(low, rotate(dkv_own, cosr[...], -sinr[...]), dkv_own).astype(BF16)
     rs_parts(3, [(gqkv, w0)])
-    dw_send([0], n1, [gqkv])
+    dw_send(0, n1, gqkv)
     rs_ring(3, lambda j: fill(f"input_{j}"))
     grad_norm_attn = rs_finish(3)
     weighted = grad_norm_attn * gain_attn
@@ -893,7 +879,7 @@
         send(ggs.at[lax.div(there * R, jnp.int32(128))], ggr.at[dev_me], p.gg_s + n, p.gg_r, to)
 
     fill("end_0")
-    swap[0] = (resid[...] + rs_direct_finish(2)).astype(BF16)
+    swap[0] = (resid[...] + rs_finish(2)).astype(BF16)
     deliver(0, block_out)
     fill("end_1")
     wait_recv(ggr.at[pl.ds(0, p.n_dev - 1)], p.gg_r)
@@ -918,6 +904,43 @@
         return carry
 
     lax.fori_loop(0, CHUNKS, last, 0)
+
+
+def unpack_kernel(
+    p, g0, g1, g2, g3, g4, rows0, rows1, o_q, o_k, o_v, o1, o2, o3, o4, out0, out1,
+    s0, s1, s2, s3, s4, s5, s6, t_q, t_k, t_v, t1, t2, t3, t4, sem,
+):
+    copies = []
+    pairs = [(g0, s0), (g2, s2), (g3, s3), (g4, s4), (g1, s1), (rows0, s5), (rows1, s6)]
+    loads = [pltpu.make_async_copy(a, b, sem.at[n]) for n, (a, b) in enumerate(pairs)]
+    for copy in loads:
+        copy.start()
+
+    def store(src, dst, n):
+        copy = pltpu.make_async_copy(src, dst, sem.at[7 + n])
+        copy.start()
+        copies.append(copy)
+
+    loads[0].wait()
+    low = lax.broadcasted_iota(jnp.int32, (1, 128), 1) < HEAD_DIM
+    for b in range(p.Z):
+        t_q[:, b * p.qc : (b + 1) * p.qc] = s0[b, :, 0 : p.qc].astype(F32)
+    for b in range(0, p.Z, 2):
+        one, two = (s0[b + n, :, p.qc : p.qc + 128].astype(F32) for n in range(2))
+        both = slice(b * HEAD_DIM, b * HEAD_DIM + 128)
+        t_k[:, both] = jnp.where(low, one, pltpu.roll(two, 64, 1))
+        t_v[:, both] = jnp.where(low, pltpu.roll(one, 64, 1), two)
+    for n, (t, o) in enumerate(((t_q, o_q), (t_k, o_k), (t_v, o_v))):
+        store(t, o, n)
+    for n, (src, t, o) in enumerate(((s2, t2, o2), (s3, t3, o3), (s4, t4, o4), (s1, t1, o1))):
+        loads[n + 1].wait()
+        t[...] = src[...].astype(F32)
+        store(t, o, n + 3)
+    for n, (src, o) in enumerate(((s5, out0), (s6, out1))):
+        loads[n + 5].wait()
+        store(src, o, n + 7)
+    for copy in copies:
+        copy.wait()
 
 
 def local(sizes, tokens, block_ids, gain_attn, w_query, key_weight, value_weight, w_out, gain_mlp,
@@ -978,7 +1001,7 @@
         pltpu.VMEM((H, model), F32),
         pltpu.VMEM((model // 128, 8, 128), F32),
         pltpu.VMEM((p.n_dev, 8, 128), F32),
-        pltpu.VMEM((2, S - 1, 2 * R, TMP), BF16),
+        pltpu.VMEM((2, S - 1, 2 * R, p.tmp), BF16),
         pltpu.SemaphoreType.DMA((p.n_send,)),
         pltpu.SemaphoreType.DMA((p.n_recv,)),
         pltpu.SemaphoreType.DMA((p.n_local,)),
@@ -997,22 +1020,25 @@
         tokens, cotangent, gin, cosine, sine, own, ids,
         w_query, key_weight, value_weight, w_out, w_gate, w_up, w_down,
     )
-    block_out, in_grad, gain_grad = outs[:3]
-    g_out, g_gate, g_up, g_down = (g.astype(F32) for g in outs[4:8])
-    g_qkv = outs[3].transpose(1, 0, 2).astype(F32)
+    gain_grad, grads = outs[2], list(outs[3:8])
+    shapes = [a.shape for a in (w_query, key_weight, value_weight, w_out, w_gate, w_up, w_down)]
+    unpacked = pl.pallas_call(
+        lambda *refs: unpack_kernel(p, *refs),
+        out_shape=[sd(a, F32) for a in shapes] + [sd((row_count, model), BF16)] * 2,
+        in_specs=[A] * 7,
+        out_specs=[A] * 9,
+        scratch_shapes=[
+            *[pltpu.VMEM(g.shape, BF16) for g in grads + list(outs[:2])],
+            *[pltpu.VMEM(a, F32) for a in shapes],
+            pltpu.SemaphoreType.DMA((16,)),
+        ],
+        compiler_params=pltpu.CompilerParams(vmem_limit_bytes=65400 * 1024),
+        name="unpack",
+    )(*grads, outs[0], outs[1])
+    g_query, g_key, g_value, g_out, g_gate, g_up, g_down, block_out, in_grad = unpacked
     gain_grads = lax.dynamic_slice(gain_grad, (0, lax.rem(ctx_me * R, 128)), (2, R))
     return (
-        block_out,
-        in_grad,
-        gain_grads[0],
-        g_qkv[:, :, : p.qc].reshape(R, -1),
-        g_qkv[:, :, p.qc : p.qc + p.kc].reshape(R, -1),
-        g_qkv[:, :, p.qc + p.kc :].reshape(R, -1),
-        g_out,
-        gain_grads[1],
-        g_gate,
-        g_up,
-        g_down,
+        block_out, in_grad, gain_grads[0], g_query, g_key, g_value, g_out, gain_grads[1], g_gate, g_up, g_down,
     )
 
 

time: 413 us -> 382 us (0.925)
  Pallas kernels: 392 us -> 374 us
  other arithmetic: 11.1 us -> 3.69 us
  local copies, waits for them, and re-layouts: 7.24 us -> 2.53 us
    pallas_call x1, Pallas kernels: 392 us -> 369 us  [local(): pl.pallas_call(lambda *refs: block_kernel(p, *refs), out_shape=out_shape,...]
    convert_element_type x5 -> x0, other arithmetic: 7.42 us -> none  [the longest x4 6.37 us: local(): g_out, g_gate, g_up, g_down = (g.astype(F32) for g in outs[4:8])]
    pallas_call x0 -> x1, Pallas kernels: none -> 4.74 us  [local(): pl.pallas_call(lambda *refs: unpack_kernel(p, *refs), out_shape=[sd(a, F3...]
where the time goes in v3:
time: 382 us; the launch traced here: 381 us
  Pallas kernels  374 us (98%)
    pallas_call x1, Pallas kernels, local(): pl.pallas_call(lambda *refs: block_kernel(p, *refs), out_shape=out_shape,...  369 us

profile of v3, /device:TPU:1, one launch (start us, length us, event | category | flops | bytes accessed | tf_op | source)
XLA Modules:
  0.0 381.3 jit_solution(16517439096545803911)
XLA Ops:
  0.7 0.1 mul.50
  0.8 1.3 fusion.4.refs_2_
  2.0 0.1 add.47
  2.1 0.7 reshape.63
  2.9 0.1 copy.24
  3.0 0.1 broadcast_in_dim_reshape.3.refs_6_
  3.1 0.0 copy-start
  3.1 0.1 add.44
  3.1 0.1 add.45
  3.2 0.6 fusion.5
  3.8 1.8 fusion
  5.6 0.0 copy-done
  5.6 369.4 %block.1 = (bf16[128,2048]{1,0:T(8,128)(2,1)}, bf16[128,2048]{1,0:T(8,128)(2,1)}, f32[8,128]{1,0:T(8,128)}, bf16[4,128,384]{2,1,0:T(8,128)(2,1)}, bf16[128,1024]...) custom-call(bf16[128,2048]{1,0:T(8,128)(2,1)} %refs_0_.1, ...), custom_call_target="tpu_custom_call" | custom-call | tf_op jit(solution)/shard_map/block/pallas_call | solution.py:1009
  375.1 1.3 slice_bitcast_fusion
  376.3 4.7 %unpack.1 = (f32[128,1024]{1,0:T(8,128)}, f32[128,256]{1,0:T(8,128)}, f32[128,256]{1,0:T(8,128)}, f32[128,1024]{1,0:T(8,128)}, f32[128,4096]{1,0:T(8,128)}, /*in...) custom-call(bf16[4,128,384]{2,1,0:T(8,128)(2,1)} %get-tuple-element.28.refs_0_, ...), custom_call_target="tpu_custom_call" | custom-call | tf_op jit(solution)/shard_map/unpack/pallas_call | solution.py:1025
  (5 shorter events, 0.0 us)
Async XLA Ops:
  3.1 2.6 copy-start

commit v4 on v3

--- a/solution.py
+++ b/solution.py
@@ -30,7 +30,9 @@
     "kv": [("forward", 1, ALL)],
     "attend_0": [("cotangent", 1)],
     "attend_1": [("cotangent", 2), ("forward", 2, ALL), ("stage", 4, ALL)],
-    "attend_2": [("cotangent", 3), ("forward", 3, ALL)],
+    "residual_0": [("cotangent", 3)],
+    "residual_1": [("forward", 3, (0, 1))],
+    "residual_3": [("forward", 3, (2, 3))],
     "n2_2": [("forward", 4, ALL)],
     "norm_0": [("grad", 4)],
     "norm_1": [("grad", 2)],
@@ -43,7 +45,8 @@
     "back_0": [("ring", 4), ("reduce", 2, (2, 3))],
     "back_1": [("reduce", 3, (0, 1))],
     "back_2": [("reduce", 3, (2, 3))],
-    "terms": [("reduce", 1, ALL)],
+    "input_0": [("reduce", 1, (0, 1))],
+    "input_1": [("reduce", 1, (2, 3))],
     "end_1": [("reduce", 0, ALL)],
 }
 

time: 382 us -> 376 us (0.984)
  Pallas kernels: 374 us -> 369 us
    pallas_call x1, Pallas kernels: 369 us -> 364 us  [local(): pl.pallas_call(lambda *refs: block_kernel(p, *refs), out_shape=out_shape,...]
where the time goes in v4:
time: 376 us
  Pallas kernels  369 us (98%)
    pallas_call x1, Pallas kernels, local(): pl.pallas_call(lambda *refs: block_kernel(p, *refs), out_shape=out_shape,...  364 us

profile of v4, /device:TPU:1, one launch (start us, length us, event | category | flops | bytes accessed | tf_op | source)
XLA Modules:
  0.0 375.6 jit_solution(5153845983031288761)
XLA Ops:
  0.7 0.1 mul.50
  0.8 1.3 fusion.4.refs_2_
  2.0 0.1 add.47
  2.1 0.7 reshape.63
  2.9 0.1 copy.24
  3.0 0.1 broadcast_in_dim_reshape.3.refs_6_
  3.1 0.0 copy-start
  3.1 0.1 add.44
  3.1 0.1 add.45
  3.2 0.6 fusion.5
  3.8 1.8 fusion
  5.6 0.0 copy-done
  5.6 363.8 %block.1 = (bf16[128,2048]{1,0:T(8,128)(2,1)}, bf16[128,2048]{1,0:T(8,128)(2,1)}, f32[8,128]{1,0:T(8,128)}, bf16[4,128,384]{2,1,0:T(8,128)(2,1)}, bf16[128,1024]...) custom-call(bf16[128,2048]{1,0:T(8,128)(2,1)} %refs_0_.1, ...), custom_call_target="tpu_custom_call" | custom-call | tf_op jit(solution)/shard_map/block/pallas_call | solution.py:1012
  369.4 1.3 slice_bitcast_fusion
  370.7 4.7 %unpack.1 = (f32[128,1024]{1,0:T(8,128)}, f32[128,256]{1,0:T(8,128)}, f32[128,256]{1,0:T(8,128)}, f32[128,1024]{1,0:T(8,128)}, f32[128,4096]{1,0:T(8,128)}, /*in...) custom-call(bf16[4,128,384]{2,1,0:T(8,128)(2,1)} %get-tuple-element.28.refs_0_, ...), custom_call_target="tpu_custom_call" | custom-call | tf_op jit(solution)/shard_map/unpack/pallas_call | solution.py:1028
  (5 shorter events, 0.0 us)
Async XLA Ops:
  3.1 2.6 copy-start
